TPU v7x, 32 devices: a whole 2x2x4 slice. The times are simulated.
32 devices in a mesh: groups: 1, ctx: 8 (over z, y), bal: 4 (over x, core), head: 1.
Axes of the slice: x: 2, y: 2, z: 4, core: 2. Of those that a mesh axis runs over, the one named last changes fastest.
Arguments:
- queries: bfloat16 [16384, 2560], P(('groups', 'ctx', 'bal'), 'head'), may hold values from -32 to 32
- keys: bfloat16 [16384, 2560], P(('groups', 'ctx', 'bal'), 'head'), may hold values from -32 to 32
- values: bfloat16 [16384, 2560], P(('groups', 'ctx', 'bal'), 'head'), may hold values from -6 to 6
- output_gradient: bfloat16 [16384, 2560], P(('groups', 'ctx', 'bal'), 'head'), may hold values from -6 to 6
- dilation_phase: int32 [20], P('head'), may hold values from 0 to 127
- segment_device_count: int32 [20], P('head'), may hold values from 1 to 32, as said below
- owner: int32 [128], P('groups'), may hold values from 0 to 127, as said below
Outputs:
- attended: bfloat16 [16384, 2560], P(('groups', 'ctx', 'bal'), 'head')
- query_grad: bfloat16 [16384, 2560], P(('groups', 'ctx', 'bal'), 'head')
- key_grad: bfloat16 [16384, 2560], P(('groups', 'ctx', 'bal'), 'head')
- value_grad: bfloat16 [16384, 2560], P(('groups', 'ctx', 'bal'), 'head')
Inputs may be any that keep to these rules, and one draw needn't show every extreme that they name: `segment_device_count`: every entry is a power of two. The device at index d of the 32 devices of a document (context shard major) holds blocks d * 4 onward. owner is one to one and keeps every block in its context shard of 4 devices: a block of the device at index b of a shard goes to some device e of that shard, into its slot b + t with 0 <= t < 1, and every device hands exactly 1 of its blocks to each device of its shard, itself included.
All inputs are finite; a program needn't handle non-finite values.
Results may differ from a plain program's by a relative error of at most 0.013.
The roundings to bfloat16 on the way count: a program that leaves them out, or rounds other values in their place, can miss the bound.
Values may be sent and summed in bfloat16 or wider, within the bound.
No kernel may reach another device: no remote copies, remote signals or barrier semaphores. Data moves between devices by JAX's collectives and lax.ppermute only.
A program may use at most 128 MiB of HBM per device.

v0:
```python
import functools
import math

import jax
import jax.numpy as jnp
from jax import lax
from jax.experimental import pallas as pl
from jax.experimental.pallas import tpu as pltpu
from jax.sharding import PartitionSpec as P

BLOCK = 128
HEAD = 128
LOG2E = 1.4426950408889634
NT = (((1,), (1,)), ((), ()))
TN = (((0,), (0,)), ((), ()))


def tables(positions, total):
    half = HEAD // 2
    pair = jnp.arange(half, dtype=jnp.float32)
    inverse = jnp.exp(pair * (-2.0 * math.log(10000.0) / HEAD))
    where = positions.astype(jnp.float32)[..., None]
    angles = where * inverse
    base = (2.0 * pair / HEAD + 0.4) / 1.4
    growth = jnp.exp((2.0 * where - total) / total * jnp.log(base))
    cosine, sine = jnp.cos(angles), jnp.sin(angles)

    def pack(scale):
        first, second = cosine * scale, sine * scale
        return (
            jnp.concatenate([first, first], axis=-1),
            jnp.concatenate([-second, second], axis=-1),
        )

    return pack(growth) + pack(1.0 / growth)


def flat_tables(positions, total):
    half = HEAD // 2
    lane = jnp.arange(positions.shape[1] * HEAD, dtype=jnp.int32) % HEAD
    pair = (lane % half).astype(jnp.float32)
    inverse = jnp.exp(pair * (-2.0 * math.log(10000.0) / HEAD))
    where = jnp.repeat(positions.astype(jnp.float32), HEAD, axis=1)
    angles = where * inverse[None, :]
    base = (2.0 * pair / HEAD + 0.4) / 1.4
    growth = jnp.exp((2.0 * where - total) / total * jnp.log(base)[None, :])
    sine = jnp.where(lane[None, :] < half, -jnp.sin(angles), jnp.sin(angles))
    return jnp.cos(angles) / growth, sine / growth


def dot(left, right, dims=None):
    if dims is None:
        dims = (((1,), (0,)), ((), ()))
    return lax.dot_general(left, right, dims, preferred_element_type=jnp.float32)


def attend_kernel(
    per_step, blocks, count, first, relaid, waits, info, phase, seg, far_ref, other_ref, pull_ref, push_ref, *rest
):
    cq_ref, sq_ref, ck_ref, sk_ref = rest[:4]
    own = rest[4:8]
    rest = rest[8:]
    if relaid:
        come, rest = rest[: blocks - 1], rest[blocks - 1 + relaid :]
        finals, rest = rest[:4], rest[4:]
    else:
        finals, rest = rest[waits : waits + blocks], rest[waits + blocks :]
    own_pay, other_pay = rest
    scale = 1.0 / math.sqrt(HEAD)
    key_at = lax.broadcasted_iota(jnp.int32, (BLOCK, BLOCK), 0)
    query_at = lax.broadcasted_iota(jnp.int32, (BLOCK, BLOCK), 1)
    far_at = lax.broadcasted_iota(jnp.int32, (count, BLOCK), 0)
    far_query = lax.broadcasted_iota(jnp.int32, (count, BLOCK), 1)
    half = HEAD // 2
    for sub in range(per_step):
        head = first + pl.program_id(0) * per_step + sub
        lanes = slice(sub * HEAD, (sub + 1) * HEAD)
        held = jnp.concatenate([far_ref[:, lanes], other_ref[:, lanes]], axis=0)
        both = dot(pull_ref[...], held).astype(jnp.bfloat16)
        far_k, far_v = both[:count], both[count:]
        span = seg[head] * blocks
        at = phase[head]
        causal = (key_at <= query_at) & (key_at != at)
        behind = far_at * BLOCK + at - far_query
        p_far, d_far, q_all, g_all = [], [], [], []
        for k in range(blocks):
            if relaid:
                rows = slice(k * BLOCK, (k + 1) * BLOCK)
                source = [ref[:, lanes] for ref in own]
                if k:
                    source = [come[k - 1][t, :, lanes] for t in range(4)]
            else:
                rows = pl.ds(pl.multiple_of(info[k] * BLOCK, BLOCK), BLOCK)
                source = [ref[rows, lanes] for ref in own]
            block = info[blocks + k]
            low = block & (-span)
            cq, sq, ck, sk = cq_ref[rows, :], sq_ref[rows, :], ck_ref[rows, :], sk_ref[rows, :]
            raw_q, raw_k, value, grad = source
            raw_q = raw_q.astype(jnp.float32)
            raw_k = raw_k.astype(jnp.float32)
            tq = (raw_q * cq + pltpu.roll(raw_q, half, 1) * sq).astype(jnp.bfloat16)
            tk = (raw_k * ck + pltpu.roll(raw_k, half, 1) * sk).astype(jnp.bfloat16)
            keys = jnp.concatenate([tk, far_k], axis=0)
            vals = jnp.concatenate([value, far_v], axis=0)
            score = dot(keys, tq, NT)
            allowed = (far_at >= low) & (behind <= block * BLOCK)
            score = jnp.concatenate(
                [
                    jnp.where(causal, score[:BLOCK], -jnp.inf),
                    jnp.where(allowed, score[BLOCK:], -jnp.inf),
                ],
                axis=0,
            )
            top = jnp.max(score, axis=0, keepdims=True)
            weight = jnp.exp2((score - top) * (scale * LOG2E))
            prob = weight * (1.0 / jnp.sum(weight, axis=0, keepdims=True))
            p16 = prob.astype(jnp.bfloat16)
            dprob = dot(vals, grad, NT)
            delta = jnp.sum(p16.astype(jnp.float32) * dprob, axis=0, keepdims=True)
            d16 = (prob * (dprob - delta)).astype(jnp.bfloat16)
            out = dot(p16, vals, TN)
            dq = dot(d16, keys, TN) * scale
            dk = dot(d16[:BLOCK], tq) * scale
            dv = dot(p16[:BLOCK], grad)
            made = (
                out,
                dq * cq - pltpu.roll(dq, half, 1) * sq,
                dk * ck - pltpu.roll(dk, half, 1) * sk,
                dv,
            )
            for t in range(4):
                if relaid:
                    finals[t][info[2 * blocks + k], :, lanes] = made[t].astype(jnp.bfloat16)
                else:
                    finals[k][t, :, lanes] = made[t].astype(jnp.bfloat16)
            p_far.append(p16[BLOCK:])
            d_far.append(d16[BLOCK:])
            q_all.append(tq)
            g_all.append(grad)
        far_dk = dot(jnp.concatenate(d_far, axis=1), jnp.concatenate(q_all, axis=0)) * scale
        far_dv = dot(jnp.concatenate(p_far, axis=1), jnp.concatenate(g_all, axis=0))
        far_sum = jnp.concatenate([far_dk, far_dv], axis=0).astype(jnp.bfloat16)
        pay = dot(push_ref[...], far_sum).astype(jnp.bfloat16)
        own_pay[:, lanes] = pay[:count]
        other_pay[:, lanes] = pay[count:]


def pick_kernel(
    heads, blocks, phase, k_hbm, v_hbm, cos_ref, sin_ref, after, out_ref, k_ref, v_ref, row_ref,
    load, save
):
    moves = [
        pltpu.make_async_copy(k_hbm, k_ref, load.at[0]),
        pltpu.make_async_copy(v_hbm, v_ref, load.at[1]),
    ]
    for move in moves:
        move.start()
    for move in moves:
        move.wait()
    spot = lax.broadcasted_iota(jnp.int32, (16, HEAD), 0)
    for head in range(heads):
        at = phase[head]
        start = pl.multiple_of(at // 16 * 16, 16)
        lanes = slice(head * HEAD, (head + 1) * HEAD)
        both = []
        for ref in (k_ref, v_ref):
            rows = []
            for k in range(blocks):
                tile = ref[pl.ds(pl.multiple_of(k * BLOCK + start, 16), 16), lanes]
                tile = jnp.where(spot == at - start, tile.astype(jnp.float32), 0.0)
                rows.append(jnp.sum(tile, axis=0, keepdims=True))
            both.append(jnp.concatenate(rows, axis=0))
        key, value = both
        key = key * cos_ref[:, lanes] + pltpu.roll(key, HEAD // 2, 1) * sin_ref[:, lanes]
        row_ref[:, lanes] = jnp.concatenate([key, value], axis=0).astype(jnp.bfloat16)
    copies = [
        pltpu.make_async_copy(row_ref, out_ref.at[d], save.at[d]) for d in range(out_ref.shape[0])
    ]
    for copy in copies:
        copy.start()
    for copy in copies:
        copy.wait()


def pack_kernel(jobs, info, after, *rest):
    number = len(jobs)
    inputs, rest = rest[:4], rest[4:]
    outs, rooms, (load, save) = rest[:number], rest[number : 2 * number], rest[2 * number :]
    order = [(job, t) for job in range(number) for t in range(4)]

    def fetch(job, t):
        k, start, width = jobs[job]
        rows = pl.ds(pl.multiple_of(info[k] * BLOCK, BLOCK), BLOCK)
        source = inputs[t].at[rows, pl.ds(start, width)]
        return pltpu.make_async_copy(source, rooms[job].at[t], load.at[job, t])

    def store(job, t):
        return pltpu.make_async_copy(rooms[job].at[t], outs[job].at[t], save.at[job, t])

    for job, t in order:
        fetch(job, t).start()
    for job, t in order:
        fetch(job, t).wait()
        store(job, t).start()
    for job, t in order:
        store(job, t).wait()


def link_kernel(*refs):
    pass


def place_kernel(items, slot, *rest):
    number = len(items)
    parts = rest[:number]
    finals = rest[number + 4 : number + 8]
    rooms, (load, save) = rest[number + 8 : 2 * number + 8], rest[2 * number + 8 :]

    def save_of(i, t):
        k, start, width = items[i]
        top = pl.multiple_of(slot[k] * BLOCK, BLOCK)
        where = finals[t].at[pl.ds(top, BLOCK), pl.ds(start, width)]
        return pltpu.make_async_copy(rooms[i].at[t], where, save.at[i, t])

    loads = [pltpu.make_async_copy(parts[i], rooms[i], load.at[i]) for i in range(number)]
    for move in loads:
        move.start()
    for i in range(number):
        loads[i].wait()
        for t in range(4):
            save_of(i, t).start()
    for i in range(number):
        for t in range(4):
            save_of(i, t).wait()


def far_rows(got, cos_ref, sin_ref, blocks):
    total = got[0].astype(jnp.float32)
    for sender in range(1, got.shape[0]):
        total = total + got[sender].astype(jnp.float32)
    far_k, far_v = total[:blocks], total[blocks:]
    heads = far_k.shape[1] // HEAD
    turned = []
    for head in range(heads):
        lanes = slice(head * HEAD, (head + 1) * HEAD)
        one = far_k[:, lanes]
        turned.append(
            one * cos_ref[:, lanes] - pltpu.roll(one, HEAD // 2, 1) * sin_ref[:, lanes]
        )
    values = [far_v[:, head * HEAD : (head + 1) * HEAD] for head in range(heads)]
    return turned, values


def overwrite(ref, lanes, at, source, pick):
    spot = lax.broadcasted_iota(jnp.int32, (16, HEAD), 0)
    line = lax.broadcasted_iota(jnp.int32, source.shape, 0)
    start = pl.multiple_of(at // 16 * 16, 16)
    row = jnp.sum(jnp.where(line == pick, source, 0.0), axis=0, keepdims=True)
    old = ref[pl.ds(start, 16), lanes].astype(jnp.float32)
    ref[pl.ds(start, 16), lanes] = jnp.where(spot == at - start, row, old).astype(jnp.bfloat16)


def patch_kernel(
    heads, blocks, late, edge, phase, slot, got_hbm, cos_ref, sin_ref, dk_in, dv_in, dk, dv, got,
    room, get, load, save
):
    outs = (dk, dv)
    width = room.shape[-1]
    order = [(k, t) for k in range(blocks) for t in range(2)]

    def span(k):
        return pl.ds(0, edge if k in late else width)

    def here(t, k):
        rows = pl.ds(pl.multiple_of(slot[k] * BLOCK, BLOCK), BLOCK)
        return outs[t].at[rows, span(k)]

    def fetch(t, k):
        return pltpu.make_async_copy(here(t, k), room.at[t, k, :, span(k)], load.at[t, k])

    def store(t, k):
        return pltpu.make_async_copy(room.at[t, k, :, span(k)], here(t, k), save.at[t, k])

    first = pltpu.make_async_copy(got_hbm, got, get)
    first.start()
    for k, t in order:
        fetch(t, k).start()
    first.wait()
    fresh = far_rows(got, cos_ref, sin_ref, blocks)
    for k, t in order:
        fetch(t, k).wait()
        for head in range(edge // HEAD if k in late else heads):
            lanes = slice(head * HEAD, (head + 1) * HEAD)
            overwrite(room.at[t, k], lanes, phase[head], fresh[t][head], slot[k])
        store(t, k).start()
    for k, t in order:
        store(t, k).wait()


def last_kernel(heads, late, edge, phase, slot, got_hbm, cos_ref, sin_ref, *rest):
    pieces = rest[:2]
    outs = rest[6:10]
    got, room, get, load, save = rest[10:]
    blocks = got.shape[1] // 2
    right = pl.ds(edge, room.shape[-1])
    rows = pl.ds(pl.multiple_of(slot[late] * BLOCK, BLOCK), BLOCK)
    first = pltpu.make_async_copy(got_hbm.at[:, :, right], got, get)
    loads, start = [], 0
    for i, piece in enumerate(pieces):
        part = pl.ds(start, piece.shape[-1])
        loads.append(pltpu.make_async_copy(piece, room.at[:, :, part], load.at[i]))
        start += piece.shape[-1]
    stores = [
        pltpu.make_async_copy(room.at[t], outs[t].at[rows, right], save.at[t]) for t in range(4)
    ]
    for move in loads + [first]:
        move.start()
    for move in loads:
        move.wait()
    for t in range(2):
        stores[t].start()
    first.wait()
    fresh = far_rows(got, cos_ref, sin_ref, blocks)
    for t in range(2):
        for head in range(edge // HEAD, heads):
            local_head = head - edge // HEAD
            lanes = slice(local_head * HEAD, (local_head + 1) * HEAD)
            overwrite(room.at[2 + t], lanes, phase[head], fresh[t][local_head], slot[late])
        stores[2 + t].start()
    for store in stores:
        store.wait()


def local(queries, keys, values, output_gradient, dilation_phase, segment_device_count, owner):
    rows, width = queries.shape
    heads = width // HEAD
    blocks = rows // BLOCK
    bal_size = lax.axis_size("bal")
    devices = lax.axis_size("ctx") * bal_size
    total = rows * devices
    count = owner.shape[0]
    assert blocks == bal_size == 4 and bal_size & (bal_size - 1) == 0
    bal = lax.axis_index("bal")
    device = lax.axis_index("ctx") * bal_size + bal
    room = 66_900_000
    big = pltpu.CompilerParams(vmem_limit_bytes=room)
    smem = pl.BlockSpec(memory_space=pltpu.SMEM)
    vmem = pl.BlockSpec(memory_space=pltpu.VMEM)
    anywhere = pl.BlockSpec(memory_space=pl.ANY)
    light = pl.CostEstimate(flops=2_000_000_000, bytes_accessed=5_000_000, transcendentals=0)
    heavy = pl.CostEstimate(flops=20_000_000_000, bytes_accessed=60_000_000, transcendentals=0)

    def tokens_of(ids):
        return (ids[:, None] * BLOCK + jnp.arange(BLOCK, dtype=jnp.int32)[None, :]).reshape(rows)

    def swap(array, k):
        return lax.ppermute(array, "bal", [(i, i ^ k) for i in range(bal_size)])

    steps = jnp.arange(blocks, dtype=jnp.int32)
    held = device * blocks + steps
    goes_to = lax.dynamic_slice_in_dim(owner, device * blocks, blocks) // blocks % bal_size
    partner = steps ^ bal
    which = jnp.sum(jnp.where(goes_to[None, :] == partner[:, None], steps[None, :], 0), axis=1)
    info = jnp.concatenate([which, device * blocks + which]).astype(jnp.int32)
    comes_from = jnp.sum(
        jnp.where(
            owner[None, :] == held[:, None], jnp.arange(count, dtype=jnp.int32)[None, :], 0
        ),
        axis=1,
    )

    first = heads * 3 // 10 * 2
    early = first // 4 * 2
    middle = heads - 2
    cut, edge, brim = early * HEAD, first * HEAD, middle * HEAD
    originals = (queries, keys, values, output_gradient)

    def send_inputs(jobs, after):
        sizes = [(4, BLOCK, width) for _, _, width in jobs]
        sent = pl.pallas_call(
            functools.partial(pack_kernel, jobs),
            in_specs=[smem] + [anywhere] * 5,
            out_specs=[anywhere] * len(jobs),
            out_shape=[jax.ShapeDtypeStruct(size, jnp.bfloat16) for size in sizes],
            scratch_shapes=[pltpu.VMEM(size, jnp.bfloat16) for size in sizes]
            + [pltpu.SemaphoreType.DMA((len(jobs), 4))] * 2,
            compiler_params=big,
        )(info, after, *originals)
        return sent, [swap(one, job[0]) for one, job in zip(sent, jobs)]

    sent, come_early = send_inputs([(2, 0, cut)], owner)

    cq, sq, ck, sk = tables(tokens_of(held), total)
    own_phase = (held[:, None] * BLOCK + dilation_phase[None, :]).astype(jnp.int32)
    pick_cos, pick_sin = flat_tables(own_phase, total)
    own_far = pl.pallas_call(
        functools.partial(pick_kernel, heads, blocks),
        in_specs=[smem, anywhere, anywhere, vmem, vmem, anywhere],
        out_specs=anywhere,
        out_shape=jax.ShapeDtypeStruct((devices // 2, 2 * blocks, width), jnp.bfloat16),
        scratch_shapes=[
            pltpu.VMEM((rows, width), jnp.bfloat16),
            pltpu.VMEM((rows, width), jnp.bfloat16),
            pltpu.VMEM((2 * blocks, width), jnp.bfloat16),
            pltpu.SemaphoreType.DMA((2,)),
            pltpu.SemaphoreType.DMA((devices // 2,)),
        ],
        compiler_params=big,
    )(
        dilation_phase,
        keys,
        values,
        pick_cos,
        pick_sin,
        sent[0],
    )
    halves = [list(range(0, devices, 2)), list(range(1, devices, 2))]
    near_far = lax.all_to_all(
        own_far,
        ("ctx", "bal"),
        split_axis=0,
        concat_axis=0,
        tiled=True,
        axis_index_groups=halves,
    ).reshape(count, width)
    other_far = swap(near_far, 1)
    jobs = [(2, cut, edge - cut), (3, 0, edge), (1, 0, edge)]
    _, (come_rest, come_3, come_1) = send_inputs(jobs, own_far)
    come_2 = come_early[0]

    ids = (device ^ steps) * blocks
    came = jnp.sum(
        jnp.where(comes_from[None, :] // blocks * blocks == ids[:, None], comes_from[None, :], 0),
        axis=1,
    )
    moved = jnp.concatenate([which, came, partner]).astype(jnp.int32)
    moved_tables = tables(tokens_of(came), total)

    side = 2 * count
    wide = jnp.arange(side, dtype=jnp.int32)
    tall = wide[:, None]
    wide = wide[None, :]
    source = tall % count
    holder = source // blocks
    held_row = (holder ^ device) % 2 * count + holder // 2 * (2 * blocks)
    pull = (wide == held_row + tall // count * blocks + source % blocks).astype(jnp.bfloat16)
    lands = owner // blocks
    lands = (lands ^ device) % 2 * count + lands // 2 * (2 * blocks) + owner % blocks
    push = (jnp.concatenate([lands, lands + blocks])[None, :] == tall).astype(jnp.bfloat16)

    per_step = 2
    columns = per_step * HEAD
    fixed = lambda h, *_: (0, 0)
    square = pl.BlockSpec((side, side), fixed)
    table = pl.BlockSpec((rows, HEAD), fixed)
    part = pl.BlockSpec((4, BLOCK, columns), lambda h, *_: (0, 0, h))
    def attend_held(begin, end, waits, carried):
        skip = begin // per_step
        tensor = pl.BlockSpec((rows, columns), lambda h, *_: (0, h + skip))
        far = pl.BlockSpec((count, columns), lambda h, *_: (0, h + skip))
        extra = carried + waits
        results = pl.pallas_call(
            functools.partial(attend_kernel, per_step, blocks, count, begin, 0, len(extra)),
            grid_spec=pltpu.PrefetchScalarGridSpec(
                num_scalar_prefetch=3,
                grid=((end - begin) // per_step,),
                in_specs=[far, far, square, square]
                + [table] * 4
                + [tensor] * 4
                + [anywhere] * len(extra),
                out_specs=[part] * blocks + [far] * 2,
            ),
            out_shape=[jax.ShapeDtypeStruct((4, BLOCK, (end - begin) * HEAD), jnp.bfloat16)]
            * blocks
            + [jax.ShapeDtypeStruct((count, width), jnp.bfloat16)] * 2,
            input_output_aliases={15 + i: blocks + i for i in range(len(carried))},
            compiler_params=big,
            cost_estimate=heavy,
        )(
            info,
            dilation_phase,
            segment_device_count,
            near_far,
            other_far,
            pull,
            push,
            cq,
            sq,
            ck,
            sk,
            *originals,
            *extra,
        )
        return list(results[:blocks]), list(results[blocks:])

    waits = list(moved_tables) + [come_1, come_2]
    parts, payload = attend_held(first, middle, waits, [])
    parts_last, payload = attend_held(middle, heads, [], payload)
    for k in range(1, blocks):
        parts[k] = swap(parts[k], k)
        parts_last[k] = swap(parts_last[k], k)

    shapes = [jax.ShapeDtypeStruct((blocks, BLOCK, width), jnp.bfloat16)] * 4
    shapes = shapes + [jax.ShapeDtypeStruct((count, width), jnp.bfloat16)] * 2

    def attend_relaid(begin, end, come, carried):
        skip = begin // per_step
        tensor = pl.BlockSpec((BLOCK, columns), lambda h, info, *_: (info[0], h + skip))
        far = pl.BlockSpec((count, columns), lambda h, *_: (0, h + skip))
        whole = pl.BlockSpec((blocks, BLOCK, columns), lambda h, *_: (0, 0, h + skip))
        shifted = pl.BlockSpec((4, BLOCK, columns), lambda h, *_: (0, 0, h + skip))
        operands = 3 + 4 + 4 + 4 + blocks - 1
        return pl.pallas_call(
            functools.partial(attend_kernel, per_step, blocks, count, begin, len(carried), 0),
            grid_spec=pltpu.PrefetchScalarGridSpec(
                num_scalar_prefetch=3,
                grid=((end - begin) // per_step,),
                in_specs=[far, far, square, square]
                + [table] * 4
                + [tensor] * 4
                + [shifted, part, shifted]
                + [anywhere] * len(carried),
                out_specs=[whole] * 4 + [far] * 2,
                ),
            out_shape=shapes,
            input_output_aliases={
                operands + i: 6 - len(carried) + i for i in range(len(carried))
            },
            compiler_params=big,
            cost_estimate=light,
        )(
            moved,
            dilation_phase,
            segment_device_count,
            near_far,
            other_far,
            pull,
            push,
            *moved_tables,
            *originals,
            *come,
            *carried,
        )

    results = attend_relaid(0, early, [come_1, come_2, come_3], payload)
    results = attend_relaid(early, first, [come_1, come_rest, come_3], results)
    finals = [one.reshape(rows, width) for one in results[:4]]

    def after(array, wait):
        return pl.pallas_call(
            link_kernel,
            in_specs=[anywhere] * 2,
            out_specs=anywhere,
            out_shape=jax.ShapeDtypeStruct(array.shape, array.dtype),
            input_output_aliases={0: 0},
            compiler_params=pltpu.CompilerParams(vmem_limit_bytes=room, has_side_effects=True),
        )(array, wait)

    crossing = swap(after(results[5], parts[2]), 1)
    payload = results[4].astype(jnp.float32) + crossing.astype(jnp.float32)
    payload = after(payload.astype(jnp.bfloat16), parts_last[2])
    got = lax.all_to_all(
        payload.reshape(devices // 2, 2 * blocks, width),
        ("ctx", "bal"),
        split_axis=0,
        concat_axis=0,
        tiled=True,
        axis_index_groups=halves,
    )

    new_phase = (comes_from[:, None] * BLOCK + dilation_phase[None, :]).astype(jnp.int32)
    new_cos, new_sin = flat_tables(new_phase, total)
    out = jax.ShapeDtypeStruct((rows, width), jnp.bfloat16)
    slots = partner.astype(jnp.int32)
    items = [(k, edge, brim - edge) for k in range(3)]
    items += [(k, brim, width - brim) for k in range(3)]
    number = len(items)
    finals = pl.pallas_call(
        functools.partial(place_kernel, items),
        in_specs=[smem] + [anywhere] * (number + 4),
        out_specs=[anywhere] * 4,
        out_shape=[out] * 4,
        input_output_aliases={1 + number + t: t for t in range(4)},
        scratch_shapes=[pltpu.VMEM((4, BLOCK, item[2]), jnp.bfloat16) for item in items]
        + [pltpu.SemaphoreType.DMA((number,)), pltpu.SemaphoreType.DMA((number, 4))],
        compiler_params=big,
        cost_estimate=light,
    )(slots, *parts[:3], *parts_last[:3], *finals)
    late = 3
    patched = pl.pallas_call(
        functools.partial(patch_kernel, heads, blocks, (late,), edge),
        in_specs=[smem, smem, anywhere, vmem, vmem, anywhere, anywhere],
        out_specs=[anywhere] * 2,
        out_shape=[out] * 2,
        input_output_aliases={5: 0, 6: 1},
        scratch_shapes=[
            pltpu.VMEM((devices // 2, 2 * blocks, width), jnp.bfloat16),
            pltpu.VMEM((2, blocks, BLOCK, width), jnp.bfloat16),
            pltpu.SemaphoreType.DMA(()),
            pltpu.SemaphoreType.DMA((2, blocks)),
            pltpu.SemaphoreType.DMA((2, blocks)),
        ],
        compiler_params=big,
        cost_estimate=light,
    )(dilation_phase, slots, got, new_cos, new_sin, finals[2], finals[3])
    return tuple(
        pl.pallas_call(
            functools.partial(last_kernel, heads, late, edge),
            in_specs=[smem, smem, anywhere, vmem, vmem] + [anywhere] * 6,
            out_specs=[anywhere] * 4,
            out_shape=[out] * 4,
            input_output_aliases={7 + t: t for t in range(4)},
            scratch_shapes=[
                pltpu.VMEM((devices // 2, 2 * blocks, width - edge), jnp.bfloat16),
                pltpu.VMEM((4, BLOCK, width - edge), jnp.bfloat16),
                pltpu.SemaphoreType.DMA(()),
                pltpu.SemaphoreType.DMA((2,)),
                pltpu.SemaphoreType.DMA((4,)),
            ],
            compiler_params=big,
        )(
            dilation_phase,
            slots,
            got,
            new_cos[:, edge:],
            new_sin[:, edge:],
            parts[late],
            parts_last[late],
            finals[0],
            finals[1],
            *patched,
        )
    )


def solution(mesh):
    token = P(("groups", "ctx", "bal"), "head")
    return jax.shard_map(
        local,
        mesh=mesh,
        in_specs=(token, token, token, token, P("head"), P("head"), P("groups")),
        out_specs=(token, token, token, token),
        check_vma=False,
    )
```

profile of v0, /device:TPU:0, one launch (start us, length us, event | category | flops | bytes accessed | tf_op | source)
XLA Modules:
  0.0 150.8 jit_solution(15956858672899724220)
XLA Ops:
  2.2 2.8 %shard_map.102.after = bf16[4,128,768]{2,1,0:T(8,128)(2,1)} custom-call(s32[8]{0:T(128)} %pad_add_fusion.2.info, s32[128]{0:T(128)} %after.1, bf16[512,2560]{1,0:T(8,128)(2,1)} %rest_4_.7, bf16[512,2560]{1,0:T(8,128)(2,1)} %rest_5_.7, bf16[512,2560]{1,0:T(8,128)(2,1)} %rest_6_.7, bf16[512,2560]{1,0:T(8,128)(2,1)} %rest_7_.7), custom_call_target="tpu_custom_call" | custom-call | tf_op jit(solution)/shard_map/pallas_call | solution.py:380
  5.0 3.0 %collective-permute-start.4 = (bf16[4,128,768]{2,1,0:T(8,128)(2,1)}, bf16[4,128,768]{2,1,0:T(8,128)(2,1)}, u32[]{:S(2)}, u32[]{:S(2)}) collective-permute-start(bf16[4,128,768]{2,1,0:T(8,128)(2,1)} %shard_map.102.after), channel_id=1, source_target_pairs={{0,2},{1,3},{2,0},{3,1},{4,6},{5,7},{6,4},{7,5},{8,10},{9,11},{10,... | collective-permute-start | bytes 2359304 | tf_op jit(solution)/shard_map/ppermute | solution.py:357
  8.5 1.3 fusion.17
  9.8 4.7 %shard_map.103.after = bf16[16,8,2560]{2,1,0:T(8,128)(2,1)} custom-call(s32[20]{0:T(128)} %phase.13, bf16[512,2560]{1,0:T(8,128)(2,1)} %rest_5_.7, bf16[512,2560]{1,0:T(8,128)(2,1)} %rest_6_.7, f32[4,2560]{1,0:T(4,128)} %get-tuple-element.76.cos_ref, f32[4,2560]{1,0:T(4,128)} %get-tuple-element.77.sin_ref, bf16[4,128,768]{2,1,0:T(8,128)(2,1)} %shard_map.102.after), custom_call_target="tpu_custom_call" | custom-call | tf_op jit(solution)/shard_map/pallas_call | solution.py:396
  14.5 6.0 %all-to-all-start = ((bf16[16,8,2560]{2,1,0:T(8,128)(2,1)}), bf16[16,8,2560]{2,1,0:T(8,128)(2,1)}, u32[]{:S(2)}, u32[]{:S(2)}) async-start(bf16[16,8,2560]{2,1,0:T(8,128)(2,1)} %shard_map.103.after), calls=%async_computation | async-start | bytes 1310720 | tf_op jit(solution)/shard_map/all_to_all | solution.py:418
  20.5 4.6 %shard_map.104 = (bf16[4,128,768]{2,1,0:T(8,128)(2,1)}, bf16[4,128,1536]{2,1,0:T(8,128)(2,1)}, bf16[4,128,1536]{2,1,0:T(8,128)(2,1)}) custom-call(s32[8]{0:T(128)} %pad_add_fusion.2.info, bf16[16,8,2560]{2,1,0:T(8,128)(2,1)} %shard_map.103.after, bf16[512,2560]{1,0:T(8,128)(2,1)} %rest_4_.7, bf16[512,2560]{1,0:T(8,128)(2,1)} %rest_5_.7, ...), custom_call_target="tpu_custom_call" | custom-call | tf_op jit(solution)/shard_map/pallas_call | solution.py:380
  25.1 2.0 %collective-permute-start.3 = (bf16[4,128,1536]{2,1,0:T(8,128)(2,1)}, bf16[4,128,1536]{2,1,0:T(8,128)(2,1)}, u32[]{:S(2)}, u32[]{:S(2)}) collective-permute-start(bf16[4,128,1536]{2,1,0:T(8,128)(2,1)} %get-tuple-element.39), channel_id=1, source_target_pairs={{0,3},{1,2},{2,1},{3,0},{4,7},{5,6},{6,5},{7,4},{8,11},{9,10},{10,... | collective-permute-start | bytes 4718600 | tf_op jit(solution)/shard_map/ppermute | solution.py:357
  27.8 2.1 %fusion.13 = (f32[512,64]{1,0:T(8,128)S(1)}, f32[512,64]{1,0:T(8,128)S(1)}, f32[512,64]{1,0:T(8,128)S(1)}, f32[512,64]{1,0:T(8,128)S(1)}, f32[512,64]{1,0:T(8,12...) fusion(f32[64]{0:T(128)S(1)} %get-tuple-element.106, ...), kind=kLoop, calls=%fused_computation.32 | loop fusion | flops 589824 | bytes 1581568 | tf_op jit(solution)/shard_map/neg | solution.py:32
  29.9 0.8 pad_maximum_fusion.rest_8_.rest_0_
  30.7 0.8 pad_maximum_fusion.2.rest_10_.rest_2_
  31.6 0.8 pad_maximum_fusion.4.rest_0_
  32.4 0.9 pad_maximum_fusion.6.rest_2_
  34.1 3.5 %all-to-all-done = bf16[16,8,2560]{2,1,0:T(8,128)(2,1)} async-done(((bf16[16,8,2560]{2,1,0:T(8,128)(2,1)}), bf16[16,8,2560]{2,1,0:T(8,128)(2,1)}, u32[]{:S(2)}, u32[]{:S(2)}) %all-to-all-start) | async-done | bytes 655392 | tf_op jit(solution)/shard_map/all_to_all | solution.py:418
  39.2 0.8 pad_maximum_fusion.7.rest_3_
  40.0 0.8 pad_maximum_fusion.1.rest_9_.rest_1_
  41.6 14.7 %shard_map.105 = (bf16[4,128,768]{2,1,0:T(8,128)(2,1)}, bf16[4,128,768]{2,1,0:T(8,128)(2,1)}, bf16[4,128,768]{2,1,0:T(8,128)(2,1)}, bf16[4,128,768]{2,1,0:T(8,12...) custom-call(s32[8]{0:T(128)} %pad_add_fusion.2.info, s32[20]{0:T(128)} %phase.13, s32[20]{0:T(128)} %seg.7, ...), custom_call_target="tpu_custom_call" | custom-call | flops 20000000000 | bytes 60000000 | tf_op jit(solution)/shard_map/pallas_call | solution.py:462
  57.0 7.0 %shard_map.106 = (bf16[4,128,256]{2,1,0:T(8,128)(2,1)}, bf16[4,128,256]{2,1,0:T(8,128)(2,1)}, bf16[4,128,256]{2,1,0:T(8,128)(2,1)}, bf16[4,128,256]{2,1,0:T(8,12...) custom-call(s32[8]{0:T(128)} %pad_add_fusion.2.info, ...), custom_call_target="tpu_custom_call", output_to_operand_aliasing={{4}: (15, {}), {5}: (16, {})} | custom-call | flops 20000000000 | bytes 60000000 | tf_op jit(solution)/shard_map/pallas_call | solution.py:462
  64.0 2.6 %collective-permute-done.3.rest_10_ = bf16[4,128,1536]{2,1,0:T(8,128)(2,1)} collective-permute-done((bf16[4,128,1536]{2,1,0:T(8,128)(2,1)}, bf16[4,128,1536]{2,1,0:T(8,128)(2,1)}, u32[]{:S(2)}, u32[]{:S(2)}) %collective-permute-start.3) | collective-permute-done | bytes 1572896 | tf_op jit(solution)/shard_map/ppermute | solution.py:357
  66.6 15.0 %shard_map.107 = (bf16[4,128,2560]{2,1,0:T(8,128)(2,1)}, bf16[4,128,2560]{2,1,0:T(8,128)(2,1)}, bf16[4,128,2560]{2,1,0:T(8,128)(2,1)}, bf16[4,128,2560]{2,1,0:T(...) custom-call(s32[12]{0:T(128)} %pad_add_fusion.1.info, ...), custom_call_target="tpu_custom_call", output_to_operand_aliasing={{4}: (18, {}), {5}: (19, {})} | custom-call | flops 2000000000 | bytes 5000000 | tf_op jit(solution)/shard_map/pallas_call | solution.py:513
  81.6 2.3 %collective-permute-done.2.rest_9_ = bf16[4,128,768]{2,1,0:T(8,128)(2,1)} collective-permute-done((bf16[4,128,768]{2,1,0:T(8,128)(2,1)}, bf16[4,128,768]{2,1,0:T(8,128)(2,1)}, u32[]{:S(2)}, u32[]{:S(2)}) %collective-permute-start.2) | collective-permute-done | bytes 786464 | tf_op jit(solution)/shard_map/ppermute | solution.py:357
  83.9 14.8 %shard_map.108 = (bf16[4,128,2560]{2,1,0:T(8,128)(2,1)}, bf16[4,128,2560]{2,1,0:T(8,128)(2,1)}, bf16[4,128,2560]{2,1,0:T(8,128)(2,1)}, bf16[4,128,2560]{2,1,0:T(...) custom-call(s32[12]{0:T(128)} %pad_add_fusion.1.info, ...), custom_call_target="tpu_custom_call", output_to_operand_aliasing={{0}: (18, {}), {1}: (19, {}), {2}: (20, {}), {3}: (21, {}),... | custom-call | flops 2000000000 | bytes 5000000 | tf_op jit(solution)/shard_map/pallas_call | solution.py:513
  98.7 1.8 %collective-permute-done.5.refs_1_.rest_2_ = bf16[4,128,768]{2,1,0:T(8,128)(2,1)} collective-permute-done((bf16[4,128,768]{2,1,0:T(8,128)(2,1)}, bf16[4,128,768]{2,1,0:T(8,128)(2,1)}, u32[]{:S(2)}, u32[]{:S(2)}) %collective-permute-start.5) | collective-permute-done | bytes 786464 | tf_op jit(solution)/shard_map/ppermute | solution.py:357
  100.6 1.5 collective-permute-start.7
  102.9 2.1 %add_convert_fusion.refs_0_ = bf16[128,2560]{1,0:T(8,128)(2,1)} fusion(bf16[128,2560]{1,0:T(8,128)(2,1)S(1)} %collective-permute-done.6, bf16[128,2560]{1,0:T(8,128)(2,1)} %get-tuple-element.50), kind=kLoop, calls=%fused_computation | loop fusion | flops 1310720 | bytes 1966080 | tf_op jit(solution)/shard_map/convert_element_type | solution.py:561
  104.9 4.6 %collective-permute-done.7.refs_1_.rest_5_ = bf16[4,128,256]{2,1,0:T(8,128)(2,1)} collective-permute-done((bf16[4,128,256]{2,1,0:T(8,128)(2,1)}, bf16[4,128,256]{2,1,0:T(8,128)(2,1)}, u32[]{:S(2)}, u32[]{:S(2)}) %collective-permute-start.7) | collective-permute-done | bytes 262176 | tf_op jit(solution)/shard_map/ppermute | solution.py:357
  109.6 6.9 %all-to-all-start.1 = ((bf16[16,8,2560]{2,1,0:T(8,128)(2,1)}), bf16[16,8,2560]{2,1,0:T(8,128)(2,1)}, u32[]{:S(2)}, u32[]{:S(2)}) async-start(bf16[16,8,2560]{2,1,0:T(8,128)(2,1)} %bitcast.56), calls=%async_computation.1 | async-start | bytes 1310720 | tf_op jit(solution)/shard_map/all_to_all | solution.py:562
  116.6 1.9 %collective-permute-start.8 = (bf16[4,128,768]{2,1,0:T(8,128)(2,1)}, bf16[4,128,768]{2,1,0:T(8,128)(2,1)}, u32[]{:S(2)}, u32[]{:S(2)}) collective-permute-start(bf16[4,128,768]{2,1,0:T(8,128)(2,1)} %get-tuple-element.54), channel_id=1, source_target_pairs={{0,3},{1,2},{2,1},{3,0},{4,7},{5,6},{6,5},{7,4},{8,11},{9,10},{10,... | collective-permute-start | bytes 2359304 | tf_op jit(solution)/shard_map/ppermute | solution.py:357
  120.4 3.7 %shard_map.111 = (bf16[512,2560]{1,0:T(8,128)(2,1)}, bf16[512,2560]{1,0:T(8,128)(2,1)}, bf16[512,2560]{1,0:T(8,128)(2,1)}, bf16[512,2560]{1,0:T(8,128)(2,1)}) custom-call(s32[4]{0:T(128)} %copy-done.3, bf16[4,128,768]{2,1,0:T(8,128)(2,1)} %get-tuple-element.56.rest_0_, ...), custom_call_target="tpu_custom_call", output_to_operand_aliasing={{0}: (7, {}), {1}: (8, {}), {2}: (9, {}), {3}: (10, {})} | custom-call | flops 2000000000 | bytes 5000000 | tf_op jit(solution)/shard_map/pallas_call | solution.py:578
  124.1 9.8 %all-to-all-done.1.got_hbm = bf16[16,8,2560]{2,1,0:T(8,128)(2,1)} async-done(((bf16[16,8,2560]{2,1,0:T(8,128)(2,1)}), bf16[16,8,2560]{2,1,0:T(8,128)(2,1)}, u32[]{:S(2)}, u32[]{:S(2)}) %all-to-all-start.1) | async-done | bytes 655392 | tf_op jit(solution)/shard_map/all_to_all | solution.py:562
  133.9 5.7 %shard_map.112 = (bf16[512,2560]{1,0:T(8,128)(2,1)}, bf16[512,2560]{1,0:T(8,128)(2,1)}) custom-call(s32[20]{0:T(128)} %phase.13, s32[4]{0:T(128)} %copy-done.3, bf16[16,8,2560]{2,1,0:T(8,128)(2,1)} %all-to-all-done.1.got_hbm, f32[4,2560]{1,0:T(4,128)} %copy-done.1, f32[4,2560]{1,0:T(4,128)} %copy-done, ...), custom_call_target="tpu_custom_call", output_to_operand_aliasing={{0}: (5, {}), {1}: (6, {})} | custom-call | flops 2000000000 | bytes 5000000 | tf_op jit(solution)/shard_map/pallas_call | solution.py:590
  139.6 8.0 %collective-permute-done.9.rest_1_ = bf16[4,128,256]{2,1,0:T(8,128)(2,1)} collective-permute-done((bf16[4,128,256]{2,1,0:T(8,128)(2,1)}, bf16[4,128,256]{2,1,0:T(8,128)(2,1)}, u32[]{:S(2)}, u32[]{:S(2)}) %collective-permute-start.9) | collective-permute-done | bytes 262176 | tf_op jit(solution)/shard_map/ppermute | solution.py:357
  147.6 3.0 %shard_map.113 = (bf16[512,2560]{1,0:T(8,128)(2,1)}, bf16[512,2560]{1,0:T(8,128)(2,1)}, bf16[512,2560]{1,0:T(8,128)(2,1)}, bf16[512,2560]{1,0:T(8,128)(2,1)}) custom-call(s32[20]{0:T(128)} %phase.13, s32[4]{0:T(128)} %copy-done.3, ...), custom_call_target="tpu_custom_call", output_to_operand_aliasing={{0}: (7, {}), {1}: (8, {}), {2}: (9, {}), {3}: (10, {})} | custom-call | tf_op jit(solution)/shard_map/pallas_call | solution.py:607
  (56 shorter events, 9.3 us)
Async XLA Ops:
  1.4 36.3 %copy-start.3 = (s32[4]{0:T(128)}, s32[4]{0:T(128)S(1)}, u32[]{:S(2)}) copy-start(s32[4]{0:T(128)S(1)} %get-tuple-element.103.slot) | copy-start | bytes 52
  2.2 5.8 %copy-start.4 = (s32[128]{0:T(128)S(1)}, s32[128]{0:T(128)}, u32[]{:S(2)}) copy-start(s32[128]{0:T(128)} %after.1) | copy-start | bytes 1540
  2.2 6.0 %copy-start.2 = (s32[20]{0:T(128)S(1)}, s32[20]{0:T(128)}, u32[]{:S(2)}) copy-start(s32[20]{0:T(128)} %phase.13) | copy-start | bytes 244
  5.0 36.6 %collective-permute-start.4 = (bf16[4,128,768]{2,1,0:T(8,128)(2,1)}, bf16[4,128,768]{2,1,0:T(8,128)(2,1)}, u32[]{:S(2)}, u32[]{:S(2)}) collective-permute-start(bf16[4,128,768]{2,1,0:T(8,128)(2,1)} %shard_map.102.after), channel_id=1, source_target_pairs={{0,2},{1,3},{2,0},{3,1},{4,6},{5,7},{6,4},{7,5},{8,10},{9,11},{10,... | collective-permute-start | bytes 2359304 | tf_op jit(solution)/shard_map/ppermute | solution.py:357
  9.8 108.8 %copy-start.1 = (f32[4,2560]{1,0:T(4,128)}, f32[4,2560]{1,0:T(4,128)S(1)}, u32[]{:S(2)}) copy-start(f32[4,2560]{1,0:T(4,128)S(1)} %get-tuple-element.73.cos_ref) | copy-start | bytes 122884
  9.8 109.4 %copy-start = (f32[4,2560]{1,0:T(4,128)}, f32[4,2560]{1,0:T(4,128)S(1)}, u32[]{:S(2)}) copy-start(f32[4,2560]{1,0:T(4,128)S(1)} %get-tuple-element.72.sin_ref) | copy-start | bytes 122884
  14.5 23.2 %all-to-all-start = ((bf16[16,8,2560]{2,1,0:T(8,128)(2,1)}), bf16[16,8,2560]{2,1,0:T(8,128)(2,1)}, u32[]{:S(2)}, u32[]{:S(2)}) async-start(bf16[16,8,2560]{2,1,0:T(8,128)(2,1)} %shard_map.103.after), calls=%async_computation | async-start | bytes 1310720 | tf_op jit(solution)/shard_map/all_to_all | solution.py:418
  25.1 16.6 %collective-permute-start.1 = (bf16[4,128,1536]{2,1,0:T(8,128)(2,1)}, bf16[4,128,1536]{2,1,0:T(8,128)(2,1)}, u32[]{:S(2)}, u32[]{:S(2)}) collective-permute-start(bf16[4,128,1536]{2,1,0:T(8,128)(2,1)} %get-tuple-element.37), channel_id=1, source_target_pairs={{0,1},{1,0},{2,3},{3,2},{4,5},{5,4},{6,7},{7,6},{8,9},{9,8},{10,11... | collective-permute-start | bytes 4718600 | tf_op jit(solution)/shard_map/ppermute | solution.py:357
  25.1 41.5 %collective-permute-start.3 = (bf16[4,128,1536]{2,1,0:T(8,128)(2,1)}, bf16[4,128,1536]{2,1,0:T(8,128)(2,1)}, u32[]{:S(2)}, u32[]{:S(2)}) collective-permute-start(bf16[4,128,1536]{2,1,0:T(8,128)(2,1)} %get-tuple-element.39), channel_id=1, source_target_pairs={{0,3},{1,2},{2,1},{3,0},{4,7},{5,6},{6,5},{7,4},{8,11},{9,10},{10,... | collective-permute-start | bytes 4718600 | tf_op jit(solution)/shard_map/ppermute | solution.py:357
  27.1 56.8 %collective-permute-start.2 = (bf16[4,128,768]{2,1,0:T(8,128)(2,1)}, bf16[4,128,768]{2,1,0:T(8,128)(2,1)}, u32[]{:S(2)}, u32[]{:S(2)}) collective-permute-start(bf16[4,128,768]{2,1,0:T(8,128)(2,1)} %get-tuple-element.38), channel_id=1, source_target_pairs={{0,2},{1,3},{2,0},{3,1},{4,6},{5,7},{6,4},{7,5},{8,10},{9,11},{10,... | collective-permute-start | bytes 2359304 | tf_op jit(solution)/shard_map/ppermute | solution.py:357
  37.7 4.0 %collective-permute-start = (bf16[128,2560]{1,0:T(8,128)(2,1)}, bf16[128,2560]{1,0:T(8,128)(2,1)}, u32[]{:S(2)}, u32[]{:S(2)}) collective-permute-start(bf16[128,2560]{1,0:T(8,128)(2,1)} %bitcast.far_ref), channel_id=1, source_target_pairs={{0,1},{1,0},{2,3},{3,2},{4,5},{5,4},{6,7},{7,6},{8,9},{9,8},{10,11... | collective-permute-start | bytes 1966088 | tf_op jit(solution)/shard_map/ppermute | solution.py:357
  56.4 44.2 %collective-permute-start.5 = (bf16[4,128,768]{2,1,0:T(8,128)(2,1)}, bf16[4,128,768]{2,1,0:T(8,128)(2,1)}, u32[]{:S(2)}, u32[]{:S(2)}) collective-permute-start(bf16[4,128,768]{2,1,0:T(8,128)(2,1)} %get-tuple-element.52), channel_id=1, source_target_pairs={{0,2},{1,3},{2,0},{3,1},{4,6},{5,7},{6,4},{7,5},{8,10},{9,11},{10,... | collective-permute-start | bytes 2359304 | tf_op jit(solution)/shard_map/ppermute | solution.py:357
  100.5 2.3 %collective-permute-start.6 = (bf16[128,2560]{1,0:T(8,128)(2,1)}, bf16[128,2560]{1,0:T(8,128)(2,1)S(1)}, u32[]{:S(2)}, u32[]{:S(2)}) collective-permute-start(bf16[128,2560]{1,0:T(8,128)(2,1)} %shard_map.109), channel_id=1, source_target_pairs={{0,1},{1,0},{2,3},{3,2},{4,5},{5,4},{6,7},{7,6},{8,9},{9,8},{10,11... | collective-permute-start | bytes 1966088 | tf_op jit(solution)/shard_map/ppermute | solution.py:357
  100.6 9.0 %collective-permute-start.7 = (bf16[4,128,256]{2,1,0:T(8,128)(2,1)}, bf16[4,128,256]{2,1,0:T(8,128)(2,1)}, u32[]{:S(2)}, u32[]{:S(2)}) collective-permute-start(bf16[4,128,256]{2,1,0:T(8,128)(2,1)} %get-tuple-element.53), channel_id=1, source_target_pairs={{0,2},{1,3},{2,0},{3,1},{4,6},{5,7},{6,4},{7,5},{8,10},{9,11},{10,... | collective-permute-start | bytes 786440 | tf_op jit(solution)/shard_map/ppermute | solution.py:357
  109.6 24.3 %all-to-all-start.1 = ((bf16[16,8,2560]{2,1,0:T(8,128)(2,1)}), bf16[16,8,2560]{2,1,0:T(8,128)(2,1)}, u32[]{:S(2)}, u32[]{:S(2)}) async-start(bf16[16,8,2560]{2,1,0:T(8,128)(2,1)} %bitcast.56), calls=%async_computation.1 | async-start | bytes 1310720 | tf_op jit(solution)/shard_map/all_to_all | solution.py:562
  116.5 3.9 %collective-permute-start.10 = (bf16[4,128,768]{2,1,0:T(8,128)(2,1)}, bf16[4,128,768]{2,1,0:T(8,128)(2,1)}, u32[]{:S(2)}, u32[]{:S(2)}) collective-permute-start(bf16[4,128,768]{2,1,0:T(8,128)(2,1)} %get-tuple-element.57), channel_id=1, source_target_pairs={{0,1},{1,0},{2,3},{3,2},{4,5},{5,4},{6,7},{7,6},{8,9},{9,8},{10,11... | collective-permute-start | bytes 2359304 | tf_op jit(solution)/shard_map/ppermute | solution.py:357
  116.6 31.0 %collective-permute-start.8 = (bf16[4,128,768]{2,1,0:T(8,128)(2,1)}, bf16[4,128,768]{2,1,0:T(8,128)(2,1)}, u32[]{:S(2)}, u32[]{:S(2)}) collective-permute-start(bf16[4,128,768]{2,1,0:T(8,128)(2,1)} %get-tuple-element.54), channel_id=1, source_target_pairs={{0,3},{1,2},{2,1},{3,0},{4,7},{5,6},{6,5},{7,4},{8,11},{9,10},{10,... | collective-permute-start | bytes 2359304 | tf_op jit(solution)/shard_map/ppermute | solution.py:357
  118.5 1.9 %collective-permute-start.11 = (bf16[4,128,256]{2,1,0:T(8,128)(2,1)}, bf16[4,128,256]{2,1,0:T(8,128)(2,1)}, u32[]{:S(2)}, u32[]{:S(2)}) collective-permute-start(bf16[4,128,256]{2,1,0:T(8,128)(2,1)} %get-tuple-element.59), channel_id=1, source_target_pairs={{0,1},{1,0},{2,3},{3,2},{4,5},{5,4},{6,7},{7,6},{8,9},{9,8},{10,11... | collective-permute-start | bytes 786440 | tf_op jit(solution)/shard_map/ppermute | solution.py:357
  119.8 27.8 %collective-permute-start.9 = (bf16[4,128,256]{2,1,0:T(8,128)(2,1)}, bf16[4,128,256]{2,1,0:T(8,128)(2,1)}, u32[]{:S(2)}, u32[]{:S(2)}) collective-permute-start(bf16[4,128,256]{2,1,0:T(8,128)(2,1)} %get-tuple-element.55), channel_id=1, source_target_pairs={{0,3},{1,2},{2,1},{3,0},{4,7},{5,6},{6,5},{7,4},{8,11},{9,10},{10,... | collective-permute-start | bytes 786440 | tf_op jit(solution)/shard_map/ppermute | solution.py:357
where the time goes:
time: 152 us; the launch traced here: 151 us
  Pallas kernels  76 us (50%)
  waiting for transfers between devices  33.9 us (22%)
  starting transfers between devices  22.6 us (15%)
  other arithmetic  16 us (11%)
    pallas_call x2, Pallas kernels, attend_relaid(): pl.pallas_call(functools.partial(attend_kernel, per_step, blocks, count,...  29.8 us
    pallas_call x2, Pallas kernels, attend_held(): pl.pallas_call(functools.partial(attend_kernel, per_step, blocks, count,...  21.7 us
    ppermute x12, waiting for transfers between devices, swap(): return lax.ppermute(array, 'bal', [(i, i ^ k) for i in range(bal_size)])  20.6 us
    all_to_all x1, waiting for transfers between devices, local(): lax.all_to_all(payload.reshape(devices // 2, 2 * blocks, width), ('ctx',...  9.8 us
    ppermute x12, starting transfers between devices, swap(): return lax.ppermute(array, 'bal', [(i, i ^ k) for i in range(bal_size)])  9.67 us
    pallas_call x2, Pallas kernels, send_inputs(): pl.pallas_call(functools.partial(pack_kernel, jobs), in_specs=[smem] + [a...  7.35 us
    all_to_all x1, starting transfers between devices, local(): lax.all_to_all(payload.reshape(devices // 2, 2 * blocks, width), ('ctx',...  6.91 us
    all_to_all x1, starting transfers between devices, local(): lax.all_to_all(own_far, ('ctx', 'bal'), split_axis=0, concat_axis=0, tile...  5.99 us
  transfers between devices with their start and end apart: 14, of which 9 were waited for; matrix products, arithmetic and copies ran while one was open for 10% of the time, Pallas kernels for 47%

commit v1 on v0

--- a/solution.py
+++ b/solution.py
@@ -182,15 +182,24 @@
         copy.wait()
 
 
-def pack_kernel(jobs, info, after, *rest):
+def pack_kernel(jobs, blocks, owner, after, *rest):
     number = len(jobs)
     inputs, rest = rest[:4], rest[4:]
     outs, rooms, (load, save) = rest[:number], rest[number : 2 * number], rest[2 * number :]
     order = [(job, t) for job in range(number) for t in range(4)]
+    bal = lax.axis_index("bal")
+    base = (lax.axis_index("ctx") * blocks + bal) * blocks
+    partners = [(owner[base + i] // blocks) % blocks ^ bal for i in range(blocks)]
+    picks = []
+    for k, _, _ in jobs:
+        pick = jnp.int32(0)
+        for i in range(1, blocks):
+            pick = jnp.where(partners[i] == k, jnp.int32(i), pick)
+        picks.append(pick)
 
     def fetch(job, t):
-        k, start, width = jobs[job]
-        rows = pl.ds(pl.multiple_of(info[k] * BLOCK, BLOCK), BLOCK)
+        _, start, width = jobs[job]
+        rows = pl.ds(pl.multiple_of(picks[job] * BLOCK, BLOCK), BLOCK)
         source = inputs[t].at[rows, pl.ds(start, width)]
         return pltpu.make_async_copy(source, rooms[job].at[t], load.at[job, t])
 
@@ -208,6 +217,10 @@
 
 def link_kernel(*refs):
     pass
+
+
+def add_kernel(left, right, after, out):
+    out[...] = (left[...].astype(jnp.float32) + right[...].astype(jnp.float32)).astype(out.dtype)
 
 
 def place_kernel(items, slot, *rest):
@@ -378,17 +391,17 @@
     def send_inputs(jobs, after):
         sizes = [(4, BLOCK, width) for _, _, width in jobs]
         sent = pl.pallas_call(
-            functools.partial(pack_kernel, jobs),
+            functools.partial(pack_kernel, jobs, blocks),
             in_specs=[smem] + [anywhere] * 5,
             out_specs=[anywhere] * len(jobs),
             out_shape=[jax.ShapeDtypeStruct(size, jnp.bfloat16) for size in sizes],
             scratch_shapes=[pltpu.VMEM(size, jnp.bfloat16) for size in sizes]
             + [pltpu.SemaphoreType.DMA((len(jobs), 4))] * 2,
             compiler_params=big,
-        )(info, after, *originals)
+        )(owner, after, *originals)
         return sent, [swap(one, job[0]) for one, job in zip(sent, jobs)]
 
-    sent, come_early = send_inputs([(2, 0, cut)], owner)
+    sent, come_early = send_inputs([(2, 0, cut)], queries)
 
     cq, sq, ck, sk = tables(tokens_of(held), total)
     own_phase = (held[:, None] * BLOCK + dilation_phase[None, :]).astype(jnp.int32)
@@ -557,8 +570,16 @@
         )(array, wait)
 
     crossing = swap(after(results[5], parts[2]), 1)
-    payload = results[4].astype(jnp.float32) + crossing.astype(jnp.float32)
-    payload = after(payload.astype(jnp.bfloat16), parts_last[2])
+    slab = pl.BlockSpec((count // 4, width), lambda i: (i, 0))
+    payload = pl.pallas_call(
+        add_kernel,
+        grid=(4,),
+        in_specs=[slab, slab, anywhere],
+        out_specs=slab,
+        out_shape=jax.ShapeDtypeStruct((count, width), jnp.bfloat16),
+        compiler_params=big,
+        cost_estimate=light,
+    )(results[4], crossing, parts_last[2])
     got = lax.all_to_all(
         payload.reshape(devices // 2, 2 * blocks, width),
         ("ctx", "bal"),

time: 152 us -> 154 us (1.013)
  Pallas kernels: 76 us -> 79.5 us
  other arithmetic: 16 us -> 13.3 us
    pallas_call x2 -> x3, Pallas kernels: 7.35 us -> 10.9 us  [the longest x2 7.44 us: send_inputs(): pl.pallas_call(functools.partial(pack_kernel, jobs, blocks), in_specs=[sm...]
    ppermute x12, waiting for transfers between devices: 20.6 us -> 22.8 us  [swap(): return lax.ppermute(array, 'bal', [(i, i ^ k) for i in range(bal_size)])]
    convert_element_type x1 -> x0, other arithmetic: 2.08 us -> none  [local(): payload = after(payload.astype(jnp.bfloat16), parts_last[2])]
  transfers between devices with their start and end apart: 14 -> 14, of which waited for: 9 -> 8; matrix products, arithmetic and copies ran while one was open for 10% -> 10% of each run, Pallas kernels for 47% -> 46%
where the time goes in v1:
time: 154 us; the launch traced here: 153 us
  Pallas kernels  79.5 us (52%)
  waiting for transfers between devices  35.1 us (23%)
  starting transfers between devices  22.5 us (15%)
  other arithmetic  13.3 us (9%)
    pallas_call x2, Pallas kernels, attend_relaid(): pl.pallas_call(functools.partial(attend_kernel, per_step, blocks, count,...  29.8 us
    ppermute x12, waiting for transfers between devices, swap(): return lax.ppermute(array, 'bal', [(i, i ^ k) for i in range(bal_size)])  22.8 us
    pallas_call x2, Pallas kernels, attend_held(): pl.pallas_call(functools.partial(attend_kernel, per_step, blocks, count,...  21.7 us
    all_to_all x1, waiting for transfers between devices, local(): lax.all_to_all(payload.reshape(devices // 2, 2 * blocks, width), ('ctx',...  9.8 us
    ppermute x12, starting transfers between devices, swap(): return lax.ppermute(array, 'bal', [(i, i ^ k) for i in range(bal_size)])  9.62 us
    pallas_call x2, Pallas kernels, send_inputs(): pl.pallas_call(functools.partial(pack_kernel, jobs, blocks), in_specs=[sm...  7.44 us
    all_to_all x1, starting transfers between devices, local(): lax.all_to_all(payload.reshape(devices // 2, 2 * blocks, width), ('ctx',...  6.85 us
    all_to_all x1, starting transfers between devices, local(): lax.all_to_all(own_far, ('ctx', 'bal'), split_axis=0, concat_axis=0, tile...  5.99 us
  transfers between devices with their start and end apart: 14, of which 8 were waited for; matrix products, arithmetic and copies ran while one was open for 10% of the time, Pallas kernels for 46%

profile of v1, /device:TPU:0, one launch (start us, length us, event | category | flops | bytes accessed | tf_op | source)
XLA Modules:
  0.0 152.7 jit_solution(9927155711964963320)
XLA Ops:
  0.7 2.8 %shard_map.102.after = bf16[4,128,768]{2,1,0:T(8,128)(2,1)} custom-call(s32[128]{0:T(128)} %owner.3, bf16[512,2560]{1,0:T(8,128)(2,1)} %rest_4_.7, bf16[512,2560]{1,0:T(8,128)(2,1)} %rest_4_.7, bf16[512,2560]{1,0:T(8,128)(2,1)} %rest_5_.7, bf16[512,2560]{1,0:T(8,128)(2,1)} %rest_6_.7, bf16[512,2560]{1,0:T(8,128)(2,1)} %rest_7_.7), custom_call_target="tpu_custom_call" | custom-call | tf_op jit(solution)/shard_map/pallas_call | solution.py:393
  3.5 3.0 %collective-permute-start.4 = (bf16[4,128,768]{2,1,0:T(8,128)(2,1)}, bf16[4,128,768]{2,1,0:T(8,128)(2,1)}, u32[]{:S(2)}, u32[]{:S(2)}) collective-permute-start(bf16[4,128,768]{2,1,0:T(8,128)(2,1)} %shard_map.102.after), channel_id=1, source_target_pairs={{0,2},{1,3},{2,0},{3,1},{4,6},{5,7},{6,4},{7,5},{8,10},{9,11},{10,... | collective-permute-start | bytes 2359304 | tf_op jit(solution)/shard_map/ppermute | solution.py:370
  7.0 1.3 fusion.17
  8.3 4.7 %shard_map.103.after = bf16[16,8,2560]{2,1,0:T(8,128)(2,1)} custom-call(s32[20]{0:T(128)} %phase.13, bf16[512,2560]{1,0:T(8,128)(2,1)} %rest_5_.7, bf16[512,2560]{1,0:T(8,128)(2,1)} %rest_6_.7, f32[4,2560]{1,0:T(4,128)} %get-tuple-element.76.cos_ref, f32[4,2560]{1,0:T(4,128)} %get-tuple-element.77.sin_ref, bf16[4,128,768]{2,1,0:T(8,128)(2,1)} %shard_map.102.after), custom_call_target="tpu_custom_call" | custom-call | tf_op jit(solution)/shard_map/pallas_call | solution.py:409
  12.9 6.0 %all-to-all-start = ((bf16[16,8,2560]{2,1,0:T(8,128)(2,1)}), bf16[16,8,2560]{2,1,0:T(8,128)(2,1)}, u32[]{:S(2)}, u32[]{:S(2)}) async-start(bf16[16,8,2560]{2,1,0:T(8,128)(2,1)} %shard_map.103.after), calls=%async_computation | async-start | bytes 1310720 | tf_op jit(solution)/shard_map/all_to_all | solution.py:431
  18.9 4.6 %shard_map.104 = (bf16[4,128,768]{2,1,0:T(8,128)(2,1)}, bf16[4,128,1536]{2,1,0:T(8,128)(2,1)}, bf16[4,128,1536]{2,1,0:T(8,128)(2,1)}) custom-call(s32[128]{0:T(128)} %owner.3, bf16[16,8,2560]{2,1,0:T(8,128)(2,1)} %shard_map.103.after, bf16[512,2560]{1,0:T(8,128)(2,1)} %rest_4_.7, bf16[512,2560]{1,0:T(8,128)(2,1)} %rest_5_.7, bf16[512,2560]{1,0:T(8,128)(2,1)} %rest_6_.7, ...), custom_call_target="tpu_custom_call" | custom-call | tf_op jit(solution)/shard_map/pallas_call | solution.py:393
  23.7 2.0 %collective-permute-start.3 = (bf16[4,128,1536]{2,1,0:T(8,128)(2,1)}, bf16[4,128,1536]{2,1,0:T(8,128)(2,1)}, u32[]{:S(2)}, u32[]{:S(2)}) collective-permute-start(bf16[4,128,1536]{2,1,0:T(8,128)(2,1)} %get-tuple-element.39), channel_id=1, source_target_pairs={{0,3},{1,2},{2,1},{3,0},{4,7},{5,6},{6,5},{7,4},{8,11},{9,10},{10,... | collective-permute-start | bytes 4718600 | tf_op jit(solution)/shard_map/ppermute | solution.py:370
  26.3 2.1 %fusion.13 = (f32[512,64]{1,0:T(8,128)S(1)}, f32[512,64]{1,0:T(8,128)S(1)}, f32[512,64]{1,0:T(8,128)S(1)}, f32[512,64]{1,0:T(8,128)S(1)}, f32[512,64]{1,0:T(8,12...) fusion(f32[64]{0:T(128)S(1)} %get-tuple-element.104, ...), kind=kLoop, calls=%fused_computation.31 | loop fusion | flops 589824 | bytes 1581568 | tf_op jit(solution)/shard_map/neg | solution.py:32
  28.4 0.8 pad_maximum_fusion.rest_8_.rest_0_
  29.6 0.8 pad_maximum_fusion.2.rest_10_.rest_2_
  30.4 0.8 pad_maximum_fusion.4.rest_0_
  31.3 0.9 pad_maximum_fusion.6.rest_2_
  33.6 2.5 %all-to-all-done = bf16[16,8,2560]{2,1,0:T(8,128)(2,1)} async-done(((bf16[16,8,2560]{2,1,0:T(8,128)(2,1)}), bf16[16,8,2560]{2,1,0:T(8,128)(2,1)}, u32[]{:S(2)}, u32[]{:S(2)}) %all-to-all-start) | async-done | bytes 655392 | tf_op jit(solution)/shard_map/all_to_all | solution.py:431
  37.6 0.8 pad_maximum_fusion.7.rest_3_
  38.5 0.8 pad_maximum_fusion.1.rest_9_.rest_1_
  40.1 14.7 %shard_map.105 = (bf16[4,128,768]{2,1,0:T(8,128)(2,1)}, bf16[4,128,768]{2,1,0:T(8,128)(2,1)}, bf16[4,128,768]{2,1,0:T(8,128)(2,1)}, bf16[4,128,768]{2,1,0:T(8,12...) custom-call(s32[8]{0:T(128)} %pad_add_fusion.2.info, s32[20]{0:T(128)} %phase.13, s32[20]{0:T(128)} %seg.7, ...), custom_call_target="tpu_custom_call" | custom-call | flops 20000000000 | bytes 60000000 | tf_op jit(solution)/shard_map/pallas_call | solution.py:475
  55.5 7.0 %shard_map.106 = (bf16[4,128,256]{2,1,0:T(8,128)(2,1)}, bf16[4,128,256]{2,1,0:T(8,128)(2,1)}, bf16[4,128,256]{2,1,0:T(8,128)(2,1)}, bf16[4,128,256]{2,1,0:T(8,12...) custom-call(s32[8]{0:T(128)} %pad_add_fusion.2.info, ...), custom_call_target="tpu_custom_call", output_to_operand_aliasing={{4}: (15, {}), {5}: (16, {})} | custom-call | flops 20000000000 | bytes 60000000 | tf_op jit(solution)/shard_map/pallas_call | solution.py:475
  62.5 2.7 %collective-permute-done.3.rest_10_ = bf16[4,128,1536]{2,1,0:T(8,128)(2,1)} collective-permute-done((bf16[4,128,1536]{2,1,0:T(8,128)(2,1)}, bf16[4,128,1536]{2,1,0:T(8,128)(2,1)}, u32[]{:S(2)}, u32[]{:S(2)}) %collective-permute-start.3) | collective-permute-done | bytes 1572896 | tf_op jit(solution)/shard_map/ppermute | solution.py:370
  65.1 15.0 %shard_map.107 = (bf16[4,128,2560]{2,1,0:T(8,128)(2,1)}, bf16[4,128,2560]{2,1,0:T(8,128)(2,1)}, bf16[4,128,2560]{2,1,0:T(8,128)(2,1)}, bf16[4,128,2560]{2,1,0:T(...) custom-call(s32[12]{0:T(128)} %pad_add_fusion.1.info, ...), custom_call_target="tpu_custom_call", output_to_operand_aliasing={{4}: (18, {}), {5}: (19, {})} | custom-call | flops 2000000000 | bytes 5000000 | tf_op jit(solution)/shard_map/pallas_call | solution.py:526
  80.1 2.3 %collective-permute-done.2.rest_9_ = bf16[4,128,768]{2,1,0:T(8,128)(2,1)} collective-permute-done((bf16[4,128,768]{2,1,0:T(8,128)(2,1)}, bf16[4,128,768]{2,1,0:T(8,128)(2,1)}, u32[]{:S(2)}, u32[]{:S(2)}) %collective-permute-start.2) | collective-permute-done | bytes 786464 | tf_op jit(solution)/shard_map/ppermute | solution.py:370
  82.4 14.8 %shard_map.108 = (bf16[4,128,2560]{2,1,0:T(8,128)(2,1)}, bf16[4,128,2560]{2,1,0:T(8,128)(2,1)}, bf16[4,128,2560]{2,1,0:T(8,128)(2,1)}, bf16[4,128,2560]{2,1,0:T(...) custom-call(s32[12]{0:T(128)} %pad_add_fusion.1.info, ...), custom_call_target="tpu_custom_call", output_to_operand_aliasing={{0}: (18, {}), {1}: (19, {}), {2}: (20, {}), {3}: (21, {}),... | custom-call | flops 2000000000 | bytes 5000000 | tf_op jit(solution)/shard_map/pallas_call | solution.py:526
  97.2 1.8 %collective-permute-done.5.refs_1_.rest_2_ = bf16[4,128,768]{2,1,0:T(8,128)(2,1)} collective-permute-done((bf16[4,128,768]{2,1,0:T(8,128)(2,1)}, bf16[4,128,768]{2,1,0:T(8,128)(2,1)}, u32[]{:S(2)}, u32[]{:S(2)}) %collective-permute-start.5) | collective-permute-done | bytes 786464 | tf_op jit(solution)/shard_map/ppermute | solution.py:370
  99.1 1.4 collective-permute-start.7
  100.5 7.6 %collective-permute-done.7.after.rest_5_ = bf16[4,128,256]{2,1,0:T(8,128)(2,1)} collective-permute-done((bf16[4,128,256]{2,1,0:T(8,128)(2,1)}, bf16[4,128,256]{2,1,0:T(8,128)(2,1)}, u32[]{:S(2)}, u32[]{:S(2)}) %collective-permute-start.7) | collective-permute-done | bytes 262176 | tf_op jit(solution)/shard_map/ppermute | solution.py:370
  108.1 3.4 %shard_map.110 = bf16[128,2560]{1,0:T(8,128)(2,1)} custom-call(bf16[128,2560]{1,0:T(8,128)(2,1)} %get-tuple-element.50.left, bf16[128,2560]{1,0:T(8,128)(2,1)} %collective-permute-done.6.right, bf16[4,128,256]{2,1,0:T(8,128)(2,1)} %collective-permute-done.7.after.rest_5_), custom_call_target="tpu_custom_call" | custom-call | flops 2000000000 | bytes 5000000 | tf_op jit(solution)/shard_map/pallas_call | solution.py:574
  111.5 6.9 %all-to-all-start.1 = ((bf16[16,8,2560]{2,1,0:T(8,128)(2,1)}), bf16[16,8,2560]{2,1,0:T(8,128)(2,1)}, u32[]{:S(2)}, u32[]{:S(2)}) async-start(bf16[16,8,2560]{2,1,0:T(8,128)(2,1)} %bitcast.56), calls=%async_computation.1 | async-start | bytes 1310720 | tf_op jit(solution)/shard_map/all_to_all | solution.py:583
  118.5 1.9 %collective-permute-start.8 = (bf16[4,128,768]{2,1,0:T(8,128)(2,1)}, bf16[4,128,768]{2,1,0:T(8,128)(2,1)}, u32[]{:S(2)}, u32[]{:S(2)}) collective-permute-start(bf16[4,128,768]{2,1,0:T(8,128)(2,1)} %get-tuple-element.54), channel_id=1, source_target_pairs={{0,3},{1,2},{2,1},{3,0},{4,7},{5,6},{6,5},{7,4},{8,11},{9,10},{10,... | collective-permute-start | bytes 2359304 | tf_op jit(solution)/shard_map/ppermute | solution.py:370
  122.3 3.7 %shard_map.111 = (bf16[512,2560]{1,0:T(8,128)(2,1)}, bf16[512,2560]{1,0:T(8,128)(2,1)}, bf16[512,2560]{1,0:T(8,128)(2,1)}, bf16[512,2560]{1,0:T(8,128)(2,1)}) custom-call(s32[4]{0:T(128)} %copy-done.5, bf16[4,128,768]{2,1,0:T(8,128)(2,1)} %get-tuple-element.56.rest_0_, ...), custom_call_target="tpu_custom_call", output_to_operand_aliasing={{0}: (7, {}), {1}: (8, {}), {2}: (9, {}), {3}: (10, {})} | custom-call | flops 2000000000 | bytes 5000000 | tf_op jit(solution)/shard_map/pallas_call | solution.py:599
  126.0 9.8 %all-to-all-done.1.got_hbm = bf16[16,8,2560]{2,1,0:T(8,128)(2,1)} async-done(((bf16[16,8,2560]{2,1,0:T(8,128)(2,1)}), bf16[16,8,2560]{2,1,0:T(8,128)(2,1)}, u32[]{:S(2)}, u32[]{:S(2)}) %all-to-all-start.1) | async-done | bytes 655392 | tf_op jit(solution)/shard_map/all_to_all | solution.py:583
  135.8 5.7 %shard_map.112 = (bf16[512,2560]{1,0:T(8,128)(2,1)}, bf16[512,2560]{1,0:T(8,128)(2,1)}) custom-call(s32[20]{0:T(128)} %phase.13, s32[4]{0:T(128)} %copy-done.5, bf16[16,8,2560]{2,1,0:T(8,128)(2,1)} %all-to-all-done.1.got_hbm, f32[4,2560]{1,0:T(4,128)} %copy-done.1, f32[4,2560]{1,0:T(4,128)} %copy-done, ...), custom_call_target="tpu_custom_call", output_to_operand_aliasing={{0}: (5, {}), {1}: (6, {})} | custom-call | flops 2000000000 | bytes 5000000 | tf_op jit(solution)/shard_map/pallas_call | solution.py:611
  141.5 8.0 %collective-permute-done.9.rest_1_ = bf16[4,128,256]{2,1,0:T(8,128)(2,1)} collective-permute-done((bf16[4,128,256]{2,1,0:T(8,128)(2,1)}, bf16[4,128,256]{2,1,0:T(8,128)(2,1)}, u32[]{:S(2)}, u32[]{:S(2)}) %collective-permute-start.9) | collective-permute-done | bytes 262176 | tf_op jit(solution)/shard_map/ppermute | solution.py:370
  149.5 3.0 %shard_map.113 = (bf16[512,2560]{1,0:T(8,128)(2,1)}, bf16[512,2560]{1,0:T(8,128)(2,1)}, bf16[512,2560]{1,0:T(8,128)(2,1)}, bf16[512,2560]{1,0:T(8,128)(2,1)}) custom-call(s32[20]{0:T(128)} %phase.13, s32[4]{0:T(128)} %copy-done.5, ...), custom_call_target="tpu_custom_call", output_to_operand_aliasing={{0}: (7, {}), {1}: (8, {}), {2}: (9, {}), {3}: (10, {})} | custom-call | tf_op jit(solution)/shard_map/pallas_call | solution.py:628
  (58 shorter events, 7.8 us)
Async XLA Ops:
  0.6 5.9 %copy-start.3 = (s32[128]{0:T(128)S(1)}, s32[128]{0:T(128)}, u32[]{:S(2)}) copy-start(s32[128]{0:T(128)} %owner.3) | copy-start | bytes 1540
  0.6 6.1 %copy-start.2 = (s32[20]{0:T(128)S(1)}, s32[20]{0:T(128)}, u32[]{:S(2)}) copy-start(s32[20]{0:T(128)} %phase.13) | copy-start | bytes 244
  3.5 36.6 %collective-permute-start.4 = (bf16[4,128,768]{2,1,0:T(8,128)(2,1)}, bf16[4,128,768]{2,1,0:T(8,128)(2,1)}, u32[]{:S(2)}, u32[]{:S(2)}) collective-permute-start(bf16[4,128,768]{2,1,0:T(8,128)(2,1)} %shard_map.102.after), channel_id=1, source_target_pairs={{0,2},{1,3},{2,0},{3,1},{4,6},{5,7},{6,4},{7,5},{8,10},{9,11},{10,... | collective-permute-start | bytes 2359304 | tf_op jit(solution)/shard_map/ppermute | solution.py:370
  8.2 112.2 %copy-start.1 = (f32[4,2560]{1,0:T(4,128)}, f32[4,2560]{1,0:T(4,128)S(1)}, u32[]{:S(2)}) copy-start(f32[4,2560]{1,0:T(4,128)S(1)} %get-tuple-element.73.cos_ref) | copy-start | bytes 122884
  8.2 112.8 %copy-start = (f32[4,2560]{1,0:T(4,128)}, f32[4,2560]{1,0:T(4,128)S(1)}, u32[]{:S(2)}) copy-start(f32[4,2560]{1,0:T(4,128)S(1)} %get-tuple-element.72.sin_ref) | copy-start | bytes 122884
  12.9 23.2 %all-to-all-start = ((bf16[16,8,2560]{2,1,0:T(8,128)(2,1)}), bf16[16,8,2560]{2,1,0:T(8,128)(2,1)}, u32[]{:S(2)}, u32[]{:S(2)}) async-start(bf16[16,8,2560]{2,1,0:T(8,128)(2,1)} %shard_map.103.after), calls=%async_computation | async-start | bytes 1310720 | tf_op jit(solution)/shard_map/all_to_all | solution.py:431
  23.6 5.7 %copy-start.4 = (s32[128]{0:T(128)S(1)}, s32[128]{0:T(128)}, u32[]{:S(2)}) copy-start(s32[128]{0:T(128)} %owner.3) | copy-start | bytes 1540
  23.6 16.5 %collective-permute-start.1 = (bf16[4,128,1536]{2,1,0:T(8,128)(2,1)}, bf16[4,128,1536]{2,1,0:T(8,128)(2,1)}, u32[]{:S(2)}, u32[]{:S(2)}) collective-permute-start(bf16[4,128,1536]{2,1,0:T(8,128)(2,1)} %get-tuple-element.37), channel_id=1, source_target_pairs={{0,1},{1,0},{2,3},{3,2},{4,5},{5,4},{6,7},{7,6},{8,9},{9,8},{10,11... | collective-permute-start | bytes 4718600 | tf_op jit(solution)/shard_map/ppermute | solution.py:370
  23.7 41.5 %collective-permute-start.3 = (bf16[4,128,1536]{2,1,0:T(8,128)(2,1)}, bf16[4,128,1536]{2,1,0:T(8,128)(2,1)}, u32[]{:S(2)}, u32[]{:S(2)}) collective-permute-start(bf16[4,128,1536]{2,1,0:T(8,128)(2,1)} %get-tuple-element.39), channel_id=1, source_target_pairs={{0,3},{1,2},{2,1},{3,0},{4,7},{5,6},{6,5},{7,4},{8,11},{9,10},{10,... | collective-permute-start | bytes 4718600 | tf_op jit(solution)/shard_map/ppermute | solution.py:370
  25.7 56.8 %collective-permute-start.2 = (bf16[4,128,768]{2,1,0:T(8,128)(2,1)}, bf16[4,128,768]{2,1,0:T(8,128)(2,1)}, u32[]{:S(2)}, u32[]{:S(2)}) collective-permute-start(bf16[4,128,768]{2,1,0:T(8,128)(2,1)} %get-tuple-element.38), channel_id=1, source_target_pairs={{0,2},{1,3},{2,0},{3,1},{4,6},{5,7},{6,4},{7,5},{8,10},{9,11},{10,... | collective-permute-start | bytes 2359304 | tf_op jit(solution)/shard_map/ppermute | solution.py:370
  26.3 6.6 %copy-start.5 = (s32[4]{0:T(128)}, s32[4]{0:T(128)S(1)}, u32[]{:S(2)}) copy-start(s32[4]{0:T(128)S(1)} %iota_xor_fusion.slot) | copy-start | bytes 52
  36.2 3.9 %collective-permute-start = (bf16[128,2560]{1,0:T(8,128)(2,1)}, bf16[128,2560]{1,0:T(8,128)(2,1)}, u32[]{:S(2)}, u32[]{:S(2)}) collective-permute-start(bf16[128,2560]{1,0:T(8,128)(2,1)} %bitcast.far_ref), channel_id=1, source_target_pairs={{0,1},{1,0},{2,3},{3,2},{4,5},{5,4},{6,7},{7,6},{8,9},{9,8},{10,11... | collective-permute-start | bytes 1966088 | tf_op jit(solution)/shard_map/ppermute | solution.py:370
  54.8 44.2 %collective-permute-start.5 = (bf16[4,128,768]{2,1,0:T(8,128)(2,1)}, bf16[4,128,768]{2,1,0:T(8,128)(2,1)}, u32[]{:S(2)}, u32[]{:S(2)}) collective-permute-start(bf16[4,128,768]{2,1,0:T(8,128)(2,1)} %get-tuple-element.52), channel_id=1, source_target_pairs={{0,2},{1,3},{2,0},{3,1},{4,6},{5,7},{6,4},{7,5},{8,10},{9,11},{10,... | collective-permute-start | bytes 2359304 | tf_op jit(solution)/shard_map/ppermute | solution.py:370
  99.1 9.0 %collective-permute-start.6 = (bf16[128,2560]{1,0:T(8,128)(2,1)}, bf16[128,2560]{1,0:T(8,128)(2,1)}, u32[]{:S(2)}, u32[]{:S(2)}) collective-permute-start(bf16[128,2560]{1,0:T(8,128)(2,1)} %shard_map.109), channel_id=1, source_target_pairs={{0,1},{1,0},{2,3},{3,2},{4,5},{5,4},{6,7},{7,6},{8,9},{9,8},{10,11... | collective-permute-start | bytes 1966088 | tf_op jit(solution)/shard_map/ppermute | solution.py:370
  99.1 9.0 %collective-permute-start.7 = (bf16[4,128,256]{2,1,0:T(8,128)(2,1)}, bf16[4,128,256]{2,1,0:T(8,128)(2,1)}, u32[]{:S(2)}, u32[]{:S(2)}) collective-permute-start(bf16[4,128,256]{2,1,0:T(8,128)(2,1)} %get-tuple-element.53), channel_id=1, source_target_pairs={{0,2},{1,3},{2,0},{3,1},{4,6},{5,7},{6,4},{7,5},{8,10},{9,11},{10,... | collective-permute-start | bytes 786440 | tf_op jit(solution)/shard_map/ppermute | solution.py:370
  111.5 24.2 %all-to-all-start.1 = ((bf16[16,8,2560]{2,1,0:T(8,128)(2,1)}), bf16[16,8,2560]{2,1,0:T(8,128)(2,1)}, u32[]{:S(2)}, u32[]{:S(2)}) async-start(bf16[16,8,2560]{2,1,0:T(8,128)(2,1)} %bitcast.56), calls=%async_computation.1 | async-start | bytes 1310720 | tf_op jit(solution)/shard_map/all_to_all | solution.py:583
  118.4 3.9 %collective-permute-start.10 = (bf16[4,128,768]{2,1,0:T(8,128)(2,1)}, bf16[4,128,768]{2,1,0:T(8,128)(2,1)}, u32[]{:S(2)}, u32[]{:S(2)}) collective-permute-start(bf16[4,128,768]{2,1,0:T(8,128)(2,1)} %get-tuple-element.57), channel_id=1, source_target_pairs={{0,1},{1,0},{2,3},{3,2},{4,5},{5,4},{6,7},{7,6},{8,9},{9,8},{10,11... | collective-permute-start | bytes 2359304 | tf_op jit(solution)/shard_map/ppermute | solution.py:370
  118.5 31.0 %collective-permute-start.8 = (bf16[4,128,768]{2,1,0:T(8,128)(2,1)}, bf16[4,128,768]{2,1,0:T(8,128)(2,1)}, u32[]{:S(2)}, u32[]{:S(2)}) collective-permute-start(bf16[4,128,768]{2,1,0:T(8,128)(2,1)} %get-tuple-element.54), channel_id=1, source_target_pairs={{0,3},{1,2},{2,1},{3,0},{4,7},{5,6},{6,5},{7,4},{8,11},{9,10},{10,... | collective-permute-start | bytes 2359304 | tf_op jit(solution)/shard_map/ppermute | solution.py:370
  120.4 1.9 %collective-permute-start.11 = (bf16[4,128,256]{2,1,0:T(8,128)(2,1)}, bf16[4,128,256]{2,1,0:T(8,128)(2,1)}, u32[]{:S(2)}, u32[]{:S(2)}) collective-permute-start(bf16[4,128,256]{2,1,0:T(8,128)(2,1)} %get-tuple-element.59), channel_id=1, source_target_pairs={{0,1},{1,0},{2,3},{3,2},{4,5},{5,4},{6,7},{7,6},{8,9},{9,8},{10,11... | collective-permute-start | bytes 786440 | tf_op jit(solution)/shard_map/ppermute | solution.py:370
  121.7 27.8 %collective-permute-start.9 = (bf16[4,128,256]{2,1,0:T(8,128)(2,1)}, bf16[4,128,256]{2,1,0:T(8,128)(2,1)}, u32[]{:S(2)}, u32[]{:S(2)}) collective-permute-start(bf16[4,128,256]{2,1,0:T(8,128)(2,1)} %get-tuple-element.55), channel_id=1, source_target_pairs={{0,3},{1,2},{2,1},{3,0},{4,7},{5,6},{6,5},{7,4},{8,11},{9,10},{10,... | collective-permute-start | bytes 786440 | tf_op jit(solution)/shard_map/ppermute | solution.py:370

commit v2 on v1

--- a/solution.py
+++ b/solution.py
@@ -219,10 +219,6 @@
     pass
 
 
-def add_kernel(left, right, after, out):
-    out[...] = (left[...].astype(jnp.float32) + right[...].astype(jnp.float32)).astype(out.dtype)
-
-
 def place_kernel(items, slot, *rest):
     number = len(items)
     parts = rest[:number]
@@ -570,16 +566,8 @@
         )(array, wait)
 
     crossing = swap(after(results[5], parts[2]), 1)
-    slab = pl.BlockSpec((count // 4, width), lambda i: (i, 0))
-    payload = pl.pallas_call(
-        add_kernel,
-        grid=(4,),
-        in_specs=[slab, slab, anywhere],
-        out_specs=slab,
-        out_shape=jax.ShapeDtypeStruct((count, width), jnp.bfloat16),
-        compiler_params=big,
-        cost_estimate=light,
-    )(results[4], crossing, parts_last[2])
+    payload = results[4].astype(jnp.float32) + crossing.astype(jnp.float32)
+    payload = after(payload.astype(jnp.bfloat16), parts_last[2])
     got = lax.all_to_all(
         payload.reshape(devices // 2, 2 * blocks, width),
         ("ctx", "bal"),

time: 154 us -> 150 us (0.974)
  Pallas kernels: 79.5 us -> 76.1 us
  waiting for transfers between devices: 35.1 us -> 33 us
  other arithmetic: 13.3 us -> 15.4 us
    pallas_call x1 -> x0, Pallas kernels: 3.43 us -> none  [local(): pl.pallas_call(add_kernel, grid=(4,), in_specs=[slab, slab, anywhere], ou...]
    ppermute x12, waiting for transfers between devices: 22.8 us -> 20.7 us  [swap(): return lax.ppermute(array, 'bal', [(i, i ^ k) for i in range(bal_size)])]
    convert_element_type x0 -> x1, other arithmetic: none -> 2.08 us  [local(): payload = after(payload.astype(jnp.bfloat16), parts_last[2])]
  transfers between devices with their start and end apart: 14 -> 14, of which waited for: 8 -> 9; matrix products, arithmetic and copies ran while one was open for 10% -> 11% of each run, Pallas kernels for 46% -> 47%
where the time goes in v2:
time: 150 us; the launch traced here: 149 us
  Pallas kernels  76.1 us (51%)
  waiting for transfers between devices  33 us (22%)
  starting transfers between devices  22.5 us (15%)
  other arithmetic  15.4 us (10%)
    pallas_call x2, Pallas kernels, attend_relaid(): pl.pallas_call(functools.partial(attend_kernel, per_step, blocks, count,...  29.8 us
    pallas_call x2, Pallas kernels, attend_held(): pl.pallas_call(functools.partial(attend_kernel, per_step, blocks, count,...  21.7 us
    ppermute x12, waiting for transfers between devices, swap(): return lax.ppermute(array, 'bal', [(i, i ^ k) for i in range(bal_size)])  20.7 us
    all_to_all x1, waiting for transfers between devices, local(): lax.all_to_all(payload.reshape(devices // 2, 2 * blocks, width), ('ctx',...  9.8 us
    ppermute x12, starting transfers between devices, swap(): return lax.ppermute(array, 'bal', [(i, i ^ k) for i in range(bal_size)])  9.62 us
    pallas_call x2, Pallas kernels, send_inputs(): pl.pallas_call(functools.partial(pack_kernel, jobs, blocks), in_specs=[sm...  7.44 us
    all_to_all x1, starting transfers between devices, local(): lax.all_to_all(payload.reshape(devices // 2, 2 * blocks, width), ('ctx',...  6.85 us
    all_to_all x1, starting transfers between devices, local(): lax.all_to_all(own_far, ('ctx', 'bal'), split_axis=0, concat_axis=0, tile...  5.99 us
  transfers between devices with their start and end apart: 14, of which 9 were waited for; matrix products, arithmetic and copies ran while one was open for 11% of the time, Pallas kernels for 47%

profile of v2, /device:TPU:0, one launch (start us, length us, event | category | flops | bytes accessed | tf_op | source)
XLA Modules:
  0.0 149.3 jit_solution(8496421573273153328)
XLA Ops:
  0.7 2.8 %shard_map.102.after = bf16[4,128,768]{2,1,0:T(8,128)(2,1)} custom-call(s32[128]{0:T(128)} %owner.3, bf16[512,2560]{1,0:T(8,128)(2,1)} %rest_4_.7, bf16[512,2560]{1,0:T(8,128)(2,1)} %rest_4_.7, bf16[512,2560]{1,0:T(8,128)(2,1)} %rest_5_.7, bf16[512,2560]{1,0:T(8,128)(2,1)} %rest_6_.7, bf16[512,2560]{1,0:T(8,128)(2,1)} %rest_7_.7), custom_call_target="tpu_custom_call" | custom-call | tf_op jit(solution)/shard_map/pallas_call | solution.py:389
  3.5 3.0 %collective-permute-start.4 = (bf16[4,128,768]{2,1,0:T(8,128)(2,1)}, bf16[4,128,768]{2,1,0:T(8,128)(2,1)}, u32[]{:S(2)}, u32[]{:S(2)}) collective-permute-start(bf16[4,128,768]{2,1,0:T(8,128)(2,1)} %shard_map.102.after), channel_id=1, source_target_pairs={{0,2},{1,3},{2,0},{3,1},{4,6},{5,7},{6,4},{7,5},{8,10},{9,11},{10,... | collective-permute-start | bytes 2359304 | tf_op jit(solution)/shard_map/ppermute | solution.py:366
  7.0 1.3 fusion.17
  8.3 4.7 %shard_map.103.after = bf16[16,8,2560]{2,1,0:T(8,128)(2,1)} custom-call(s32[20]{0:T(128)} %phase.13, bf16[512,2560]{1,0:T(8,128)(2,1)} %rest_5_.7, bf16[512,2560]{1,0:T(8,128)(2,1)} %rest_6_.7, f32[4,2560]{1,0:T(4,128)} %get-tuple-element.76.cos_ref, f32[4,2560]{1,0:T(4,128)} %get-tuple-element.77.sin_ref, bf16[4,128,768]{2,1,0:T(8,128)(2,1)} %shard_map.102.after), custom_call_target="tpu_custom_call" | custom-call | tf_op jit(solution)/shard_map/pallas_call | solution.py:405
  12.9 6.0 %all-to-all-start = ((bf16[16,8,2560]{2,1,0:T(8,128)(2,1)}), bf16[16,8,2560]{2,1,0:T(8,128)(2,1)}, u32[]{:S(2)}, u32[]{:S(2)}) async-start(bf16[16,8,2560]{2,1,0:T(8,128)(2,1)} %shard_map.103.after), calls=%async_computation | async-start | bytes 1310720 | tf_op jit(solution)/shard_map/all_to_all | solution.py:427
  18.9 4.6 %shard_map.104 = (bf16[4,128,768]{2,1,0:T(8,128)(2,1)}, bf16[4,128,1536]{2,1,0:T(8,128)(2,1)}, bf16[4,128,1536]{2,1,0:T(8,128)(2,1)}) custom-call(s32[128]{0:T(128)} %owner.3, bf16[16,8,2560]{2,1,0:T(8,128)(2,1)} %shard_map.103.after, bf16[512,2560]{1,0:T(8,128)(2,1)} %rest_4_.7, bf16[512,2560]{1,0:T(8,128)(2,1)} %rest_5_.7, bf16[512,2560]{1,0:T(8,128)(2,1)} %rest_6_.7, ...), custom_call_target="tpu_custom_call" | custom-call | tf_op jit(solution)/shard_map/pallas_call | solution.py:389
  23.7 2.0 %collective-permute-start.3 = (bf16[4,128,1536]{2,1,0:T(8,128)(2,1)}, bf16[4,128,1536]{2,1,0:T(8,128)(2,1)}, u32[]{:S(2)}, u32[]{:S(2)}) collective-permute-start(bf16[4,128,1536]{2,1,0:T(8,128)(2,1)} %get-tuple-element.39), channel_id=1, source_target_pairs={{0,3},{1,2},{2,1},{3,0},{4,7},{5,6},{6,5},{7,4},{8,11},{9,10},{10,... | collective-permute-start | bytes 4718600 | tf_op jit(solution)/shard_map/ppermute | solution.py:366
  26.3 2.1 %fusion.13 = (f32[512,64]{1,0:T(8,128)S(1)}, f32[512,64]{1,0:T(8,128)S(1)}, f32[512,64]{1,0:T(8,128)S(1)}, f32[512,64]{1,0:T(8,128)S(1)}, f32[512,64]{1,0:T(8,12...) fusion(f32[64]{0:T(128)S(1)} %get-tuple-element.104, ...), kind=kLoop, calls=%fused_computation.32 | loop fusion | flops 589824 | bytes 1581568 | tf_op jit(solution)/shard_map/neg | solution.py:32
  28.4 0.8 pad_maximum_fusion.rest_8_.rest_0_
  30.4 0.8 pad_maximum_fusion.4.rest_0_
  31.3 0.9 pad_maximum_fusion.6.rest_2_
  33.6 2.5 %all-to-all-done = bf16[16,8,2560]{2,1,0:T(8,128)(2,1)} async-done(((bf16[16,8,2560]{2,1,0:T(8,128)(2,1)}), bf16[16,8,2560]{2,1,0:T(8,128)(2,1)}, u32[]{:S(2)}, u32[]{:S(2)}) %all-to-all-start) | async-done | bytes 655392 | tf_op jit(solution)/shard_map/all_to_all | solution.py:427
  37.6 0.8 pad_maximum_fusion.7.rest_3_
  38.5 0.8 pad_maximum_fusion.1.rest_9_.rest_1_
  40.1 14.7 %shard_map.105 = (bf16[4,128,768]{2,1,0:T(8,128)(2,1)}, bf16[4,128,768]{2,1,0:T(8,128)(2,1)}, bf16[4,128,768]{2,1,0:T(8,128)(2,1)}, bf16[4,128,768]{2,1,0:T(8,12...) custom-call(s32[8]{0:T(128)} %pad_add_fusion.2.info, s32[20]{0:T(128)} %phase.13, s32[20]{0:T(128)} %seg.7, ...), custom_call_target="tpu_custom_call" | custom-call | flops 20000000000 | bytes 60000000 | tf_op jit(solution)/shard_map/pallas_call | solution.py:471
  55.5 7.0 %shard_map.106 = (bf16[4,128,256]{2,1,0:T(8,128)(2,1)}, bf16[4,128,256]{2,1,0:T(8,128)(2,1)}, bf16[4,128,256]{2,1,0:T(8,128)(2,1)}, bf16[4,128,256]{2,1,0:T(8,12...) custom-call(s32[8]{0:T(128)} %pad_add_fusion.2.info, ...), custom_call_target="tpu_custom_call", output_to_operand_aliasing={{4}: (15, {}), {5}: (16, {})} | custom-call | flops 20000000000 | bytes 60000000 | tf_op jit(solution)/shard_map/pallas_call | solution.py:471
  62.5 2.7 %collective-permute-done.3.rest_10_ = bf16[4,128,1536]{2,1,0:T(8,128)(2,1)} collective-permute-done((bf16[4,128,1536]{2,1,0:T(8,128)(2,1)}, bf16[4,128,1536]{2,1,0:T(8,128)(2,1)}, u32[]{:S(2)}, u32[]{:S(2)}) %collective-permute-start.3) | collective-permute-done | bytes 1572896 | tf_op jit(solution)/shard_map/ppermute | solution.py:366
  65.1 15.0 %shard_map.107 = (bf16[4,128,2560]{2,1,0:T(8,128)(2,1)}, bf16[4,128,2560]{2,1,0:T(8,128)(2,1)}, bf16[4,128,2560]{2,1,0:T(8,128)(2,1)}, bf16[4,128,2560]{2,1,0:T(...) custom-call(s32[12]{0:T(128)} %pad_add_fusion.1.info, ...), custom_call_target="tpu_custom_call", output_to_operand_aliasing={{4}: (18, {}), {5}: (19, {})} | custom-call | flops 2000000000 | bytes 5000000 | tf_op jit(solution)/shard_map/pallas_call | solution.py:522
  80.1 2.3 %collective-permute-done.2.rest_9_ = bf16[4,128,768]{2,1,0:T(8,128)(2,1)} collective-permute-done((bf16[4,128,768]{2,1,0:T(8,128)(2,1)}, bf16[4,128,768]{2,1,0:T(8,128)(2,1)}, u32[]{:S(2)}, u32[]{:S(2)}) %collective-permute-start.2) | collective-permute-done | bytes 786464 | tf_op jit(solution)/shard_map/ppermute | solution.py:366
  82.4 14.8 %shard_map.108 = (bf16[4,128,2560]{2,1,0:T(8,128)(2,1)}, bf16[4,128,2560]{2,1,0:T(8,128)(2,1)}, bf16[4,128,2560]{2,1,0:T(8,128)(2,1)}, bf16[4,128,2560]{2,1,0:T(...) custom-call(s32[12]{0:T(128)} %pad_add_fusion.1.info, ...), custom_call_target="tpu_custom_call", output_to_operand_aliasing={{0}: (18, {}), {1}: (19, {}), {2}: (20, {}), {3}: (21, {}),... | custom-call | flops 2000000000 | bytes 5000000 | tf_op jit(solution)/shard_map/pallas_call | solution.py:522
  97.2 1.8 %collective-permute-done.5.refs_1_.rest_2_ = bf16[4,128,768]{2,1,0:T(8,128)(2,1)} collective-permute-done((bf16[4,128,768]{2,1,0:T(8,128)(2,1)}, bf16[4,128,768]{2,1,0:T(8,128)(2,1)}, u32[]{:S(2)}, u32[]{:S(2)}) %collective-permute-start.5) | collective-permute-done | bytes 786464 | tf_op jit(solution)/shard_map/ppermute | solution.py:366
  99.1 1.4 collective-permute-start.7
  100.5 0.9 collective-permute-done.6
  101.4 2.1 %add_convert_fusion.refs_0_ = bf16[128,2560]{1,0:T(8,128)(2,1)} fusion(bf16[128,2560]{1,0:T(8,128)(2,1)S(1)} %collective-permute-done.6, bf16[128,2560]{1,0:T(8,128)(2,1)} %get-tuple-element.50), kind=kLoop, calls=%fused_computation | loop fusion | flops 1310720 | bytes 1966080 | tf_op jit(solution)/shard_map/convert_element_type | solution.py:570
  103.5 4.6 %collective-permute-done.7.refs_1_.rest_5_ = bf16[4,128,256]{2,1,0:T(8,128)(2,1)} collective-permute-done((bf16[4,128,256]{2,1,0:T(8,128)(2,1)}, bf16[4,128,256]{2,1,0:T(8,128)(2,1)}, u32[]{:S(2)}, u32[]{:S(2)}) %collective-permute-start.7) | collective-permute-done | bytes 262176 | tf_op jit(solution)/shard_map/ppermute | solution.py:366
  108.1 6.9 %all-to-all-start.1 = ((bf16[16,8,2560]{2,1,0:T(8,128)(2,1)}), bf16[16,8,2560]{2,1,0:T(8,128)(2,1)}, u32[]{:S(2)}, u32[]{:S(2)}) async-start(bf16[16,8,2560]{2,1,0:T(8,128)(2,1)} %bitcast.56), calls=%async_computation.1 | async-start | bytes 1310720 | tf_op jit(solution)/shard_map/all_to_all | solution.py:571
  115.1 1.9 %collective-permute-start.8 = (bf16[4,128,768]{2,1,0:T(8,128)(2,1)}, bf16[4,128,768]{2,1,0:T(8,128)(2,1)}, u32[]{:S(2)}, u32[]{:S(2)}) collective-permute-start(bf16[4,128,768]{2,1,0:T(8,128)(2,1)} %get-tuple-element.54), channel_id=1, source_target_pairs={{0,3},{1,2},{2,1},{3,0},{4,7},{5,6},{6,5},{7,4},{8,11},{9,10},{10,... | collective-permute-start | bytes 2359304 | tf_op jit(solution)/shard_map/ppermute | solution.py:366
  118.8 3.7 %shard_map.111 = (bf16[512,2560]{1,0:T(8,128)(2,1)}, bf16[512,2560]{1,0:T(8,128)(2,1)}, bf16[512,2560]{1,0:T(8,128)(2,1)}, bf16[512,2560]{1,0:T(8,128)(2,1)}) custom-call(s32[4]{0:T(128)} %copy-done.5, bf16[4,128,768]{2,1,0:T(8,128)(2,1)} %get-tuple-element.56.rest_0_, ...), custom_call_target="tpu_custom_call", output_to_operand_aliasing={{0}: (7, {}), {1}: (8, {}), {2}: (9, {}), {3}: (10, {})} | custom-call | flops 2000000000 | bytes 5000000 | tf_op jit(solution)/shard_map/pallas_call | solution.py:587
  122.6 9.8 %all-to-all-done.1.got_hbm = bf16[16,8,2560]{2,1,0:T(8,128)(2,1)} async-done(((bf16[16,8,2560]{2,1,0:T(8,128)(2,1)}), bf16[16,8,2560]{2,1,0:T(8,128)(2,1)}, u32[]{:S(2)}, u32[]{:S(2)}) %all-to-all-start.1) | async-done | bytes 655392 | tf_op jit(solution)/shard_map/all_to_all | solution.py:571
  132.4 5.7 %shard_map.112 = (bf16[512,2560]{1,0:T(8,128)(2,1)}, bf16[512,2560]{1,0:T(8,128)(2,1)}) custom-call(s32[20]{0:T(128)} %phase.13, s32[4]{0:T(128)} %copy-done.5, bf16[16,8,2560]{2,1,0:T(8,128)(2,1)} %all-to-all-done.1.got_hbm, f32[4,2560]{1,0:T(4,128)} %copy-done.1, f32[4,2560]{1,0:T(4,128)} %copy-done, ...), custom_call_target="tpu_custom_call", output_to_operand_aliasing={{0}: (5, {}), {1}: (6, {})} | custom-call | flops 2000000000 | bytes 5000000 | tf_op jit(solution)/shard_map/pallas_call | solution.py:599
  138.1 8.0 %collective-permute-done.9.rest_1_ = bf16[4,128,256]{2,1,0:T(8,128)(2,1)} collective-permute-done((bf16[4,128,256]{2,1,0:T(8,128)(2,1)}, bf16[4,128,256]{2,1,0:T(8,128)(2,1)}, u32[]{:S(2)}, u32[]{:S(2)}) %collective-permute-start.9) | collective-permute-done | bytes 262176 | tf_op jit(solution)/shard_map/ppermute | solution.py:366
  146.1 3.0 %shard_map.113 = (bf16[512,2560]{1,0:T(8,128)(2,1)}, bf16[512,2560]{1,0:T(8,128)(2,1)}, bf16[512,2560]{1,0:T(8,128)(2,1)}, bf16[512,2560]{1,0:T(8,128)(2,1)}) custom-call(s32[20]{0:T(128)} %phase.13, s32[4]{0:T(128)} %copy-done.5, ...), custom_call_target="tpu_custom_call", output_to_operand_aliasing={{0}: (7, {}), {1}: (8, {}), {2}: (9, {}), {3}: (10, {})} | custom-call | tf_op jit(solution)/shard_map/pallas_call | solution.py:616
  (59 shorter events, 8.7 us)
Async XLA Ops:
  0.6 5.9 %copy-start.3 = (s32[128]{0:T(128)S(1)}, s32[128]{0:T(128)}, u32[]{:S(2)}) copy-start(s32[128]{0:T(128)} %owner.3) | copy-start | bytes 1540
  0.6 6.1 %copy-start.2 = (s32[20]{0:T(128)S(1)}, s32[20]{0:T(128)}, u32[]{:S(2)}) copy-start(s32[20]{0:T(128)} %phase.13) | copy-start | bytes 244
  3.5 36.6 %collective-permute-start.4 = (bf16[4,128,768]{2,1,0:T(8,128)(2,1)}, bf16[4,128,768]{2,1,0:T(8,128)(2,1)}, u32[]{:S(2)}, u32[]{:S(2)}) collective-permute-start(bf16[4,128,768]{2,1,0:T(8,128)(2,1)} %shard_map.102.after), channel_id=1, source_target_pairs={{0,2},{1,3},{2,0},{3,1},{4,6},{5,7},{6,4},{7,5},{8,10},{9,11},{10,... | collective-permute-start | bytes 2359304 | tf_op jit(solution)/shard_map/ppermute | solution.py:366
  8.2 108.8 %copy-start.1 = (f32[4,2560]{1,0:T(4,128)}, f32[4,2560]{1,0:T(4,128)S(1)}, u32[]{:S(2)}) copy-start(f32[4,2560]{1,0:T(4,128)S(1)} %get-tuple-element.73.cos_ref) | copy-start | bytes 122884
  8.2 109.4 %copy-start = (f32[4,2560]{1,0:T(4,128)}, f32[4,2560]{1,0:T(4,128)S(1)}, u32[]{:S(2)}) copy-start(f32[4,2560]{1,0:T(4,128)S(1)} %get-tuple-element.72.sin_ref) | copy-start | bytes 122884
  12.9 23.2 %all-to-all-start = ((bf16[16,8,2560]{2,1,0:T(8,128)(2,1)}), bf16[16,8,2560]{2,1,0:T(8,128)(2,1)}, u32[]{:S(2)}, u32[]{:S(2)}) async-start(bf16[16,8,2560]{2,1,0:T(8,128)(2,1)} %shard_map.103.after), calls=%async_computation | async-start | bytes 1310720 | tf_op jit(solution)/shard_map/all_to_all | solution.py:427
  23.6 5.7 %copy-start.4 = (s32[128]{0:T(128)S(1)}, s32[128]{0:T(128)}, u32[]{:S(2)}) copy-start(s32[128]{0:T(128)} %owner.3) | copy-start | bytes 1540
  23.6 16.5 %collective-permute-start.1 = (bf16[4,128,1536]{2,1,0:T(8,128)(2,1)}, bf16[4,128,1536]{2,1,0:T(8,128)(2,1)}, u32[]{:S(2)}, u32[]{:S(2)}) collective-permute-start(bf16[4,128,1536]{2,1,0:T(8,128)(2,1)} %get-tuple-element.37), channel_id=1, source_target_pairs={{0,1},{1,0},{2,3},{3,2},{4,5},{5,4},{6,7},{7,6},{8,9},{9,8},{10,11... | collective-permute-start | bytes 4718600 | tf_op jit(solution)/shard_map/ppermute | solution.py:366
  23.7 41.5 %collective-permute-start.3 = (bf16[4,128,1536]{2,1,0:T(8,128)(2,1)}, bf16[4,128,1536]{2,1,0:T(8,128)(2,1)}, u32[]{:S(2)}, u32[]{:S(2)}) collective-permute-start(bf16[4,128,1536]{2,1,0:T(8,128)(2,1)} %get-tuple-element.39), channel_id=1, source_target_pairs={{0,3},{1,2},{2,1},{3,0},{4,7},{5,6},{6,5},{7,4},{8,11},{9,10},{10,... | collective-permute-start | bytes 4718600 | tf_op jit(solution)/shard_map/ppermute | solution.py:366
  25.7 56.8 %collective-permute-start.2 = (bf16[4,128,768]{2,1,0:T(8,128)(2,1)}, bf16[4,128,768]{2,1,0:T(8,128)(2,1)}, u32[]{:S(2)}, u32[]{:S(2)}) collective-permute-start(bf16[4,128,768]{2,1,0:T(8,128)(2,1)} %get-tuple-element.38), channel_id=1, source_target_pairs={{0,2},{1,3},{2,0},{3,1},{4,6},{5,7},{6,4},{7,5},{8,10},{9,11},{10,... | collective-permute-start | bytes 2359304 | tf_op jit(solution)/shard_map/ppermute | solution.py:366
  26.3 6.6 %copy-start.5 = (s32[4]{0:T(128)}, s32[4]{0:T(128)S(1)}, u32[]{:S(2)}) copy-start(s32[4]{0:T(128)S(1)} %iota_xor_fusion.slot) | copy-start | bytes 52
  36.2 3.9 %collective-permute-start = (bf16[128,2560]{1,0:T(8,128)(2,1)}, bf16[128,2560]{1,0:T(8,128)(2,1)}, u32[]{:S(2)}, u32[]{:S(2)}) collective-permute-start(bf16[128,2560]{1,0:T(8,128)(2,1)} %bitcast.far_ref), channel_id=1, source_target_pairs={{0,1},{1,0},{2,3},{3,2},{4,5},{5,4},{6,7},{7,6},{8,9},{9,8},{10,11... | collective-permute-start | bytes 1966088 | tf_op jit(solution)/shard_map/ppermute | solution.py:366
  54.8 44.2 %collective-permute-start.5 = (bf16[4,128,768]{2,1,0:T(8,128)(2,1)}, bf16[4,128,768]{2,1,0:T(8,128)(2,1)}, u32[]{:S(2)}, u32[]{:S(2)}) collective-permute-start(bf16[4,128,768]{2,1,0:T(8,128)(2,1)} %get-tuple-element.52), channel_id=1, source_target_pairs={{0,2},{1,3},{2,0},{3,1},{4,6},{5,7},{6,4},{7,5},{8,10},{9,11},{10,... | collective-permute-start | bytes 2359304 | tf_op jit(solution)/shard_map/ppermute | solution.py:366
  99.1 2.3 %collective-permute-start.6 = (bf16[128,2560]{1,0:T(8,128)(2,1)}, bf16[128,2560]{1,0:T(8,128)(2,1)S(1)}, u32[]{:S(2)}, u32[]{:S(2)}) collective-permute-start(bf16[128,2560]{1,0:T(8,128)(2,1)} %shard_map.109), channel_id=1, source_target_pairs={{0,1},{1,0},{2,3},{3,2},{4,5},{5,4},{6,7},{7,6},{8,9},{9,8},{10,11... | collective-permute-start | bytes 1966088 | tf_op jit(solution)/shard_map/ppermute | solution.py:366
  99.1 9.0 %collective-permute-start.7 = (bf16[4,128,256]{2,1,0:T(8,128)(2,1)}, bf16[4,128,256]{2,1,0:T(8,128)(2,1)}, u32[]{:S(2)}, u32[]{:S(2)}) collective-permute-start(bf16[4,128,256]{2,1,0:T(8,128)(2,1)} %get-tuple-element.53), channel_id=1, source_target_pairs={{0,2},{1,3},{2,0},{3,1},{4,6},{5,7},{6,4},{7,5},{8,10},{9,11},{10,... | collective-permute-start | bytes 786440 | tf_op jit(solution)/shard_map/ppermute | solution.py:366
  108.1 24.2 %all-to-all-start.1 = ((bf16[16,8,2560]{2,1,0:T(8,128)(2,1)}), bf16[16,8,2560]{2,1,0:T(8,128)(2,1)}, u32[]{:S(2)}, u32[]{:S(2)}) async-start(bf16[16,8,2560]{2,1,0:T(8,128)(2,1)} %bitcast.56), calls=%async_computation.1 | async-start | bytes 1310720 | tf_op jit(solution)/shard_map/all_to_all | solution.py:571
  115.0 3.9 %collective-permute-start.10 = (bf16[4,128,768]{2,1,0:T(8,128)(2,1)}, bf16[4,128,768]{2,1,0:T(8,128)(2,1)}, u32[]{:S(2)}, u32[]{:S(2)}) collective-permute-start(bf16[4,128,768]{2,1,0:T(8,128)(2,1)} %get-tuple-element.57), channel_id=1, source_target_pairs={{0,1},{1,0},{2,3},{3,2},{4,5},{5,4},{6,7},{7,6},{8,9},{9,8},{10,11... | collective-permute-start | bytes 2359304 | tf_op jit(solution)/shard_map/ppermute | solution.py:366
  115.1 31.0 %collective-permute-start.8 = (bf16[4,128,768]{2,1,0:T(8,128)(2,1)}, bf16[4,128,768]{2,1,0:T(8,128)(2,1)}, u32[]{:S(2)}, u32[]{:S(2)}) collective-permute-start(bf16[4,128,768]{2,1,0:T(8,128)(2,1)} %get-tuple-element.54), channel_id=1, source_target_pairs={{0,3},{1,2},{2,1},{3,0},{4,7},{5,6},{6,5},{7,4},{8,11},{9,10},{10,... | collective-permute-start | bytes 2359304 | tf_op jit(solution)/shard_map/ppermute | solution.py:366
  117.0 1.9 %collective-permute-start.11 = (bf16[4,128,256]{2,1,0:T(8,128)(2,1)}, bf16[4,128,256]{2,1,0:T(8,128)(2,1)}, u32[]{:S(2)}, u32[]{:S(2)}) collective-permute-start(bf16[4,128,256]{2,1,0:T(8,128)(2,1)} %get-tuple-element.59), channel_id=1, source_target_pairs={{0,1},{1,0},{2,3},{3,2},{4,5},{5,4},{6,7},{7,6},{8,9},{9,8},{10,11... | collective-permute-start | bytes 786440 | tf_op jit(solution)/shard_map/ppermute | solution.py:366
  118.3 27.8 %collective-permute-start.9 = (bf16[4,128,256]{2,1,0:T(8,128)(2,1)}, bf16[4,128,256]{2,1,0:T(8,128)(2,1)}, u32[]{:S(2)}, u32[]{:S(2)}) collective-permute-start(bf16[4,128,256]{2,1,0:T(8,128)(2,1)} %get-tuple-element.55), channel_id=1, source_target_pairs={{0,3},{1,2},{2,1},{3,0},{4,7},{5,6},{6,5},{7,4},{8,11},{9,10},{10,... | collective-permute-start | bytes 786440 | tf_op jit(solution)/shard_map/ppermute | solution.py:366

commit v3 on v2

--- a/solution.py
+++ b/solution.py
@@ -306,35 +306,29 @@
         store(t, k).wait()
 
 
-def last_kernel(heads, late, edge, phase, slot, got_hbm, cos_ref, sin_ref, *rest):
-    pieces = rest[:2]
-    outs = rest[6:10]
-    got, room, get, load, save = rest[10:]
+def last_kernel(late, begin, end, phase, slot, got_hbm, cos_ref, sin_ref, piece, *rest):
+    outs = rest[4:8]
+    got, room, get, load, save = rest[8:]
     blocks = got.shape[1] // 2
-    right = pl.ds(edge, room.shape[-1])
+    right = pl.ds(begin * HEAD, room.shape[-1])
     rows = pl.ds(pl.multiple_of(slot[late] * BLOCK, BLOCK), BLOCK)
     first = pltpu.make_async_copy(got_hbm.at[:, :, right], got, get)
-    loads, start = [], 0
-    for i, piece in enumerate(pieces):
-        part = pl.ds(start, piece.shape[-1])
-        loads.append(pltpu.make_async_copy(piece, room.at[:, :, part], load.at[i]))
-        start += piece.shape[-1]
+    whole = pltpu.make_async_copy(piece, room, load)
     stores = [
         pltpu.make_async_copy(room.at[t], outs[t].at[rows, right], save.at[t]) for t in range(4)
     ]
-    for move in loads + [first]:
-        move.start()
-    for move in loads:
-        move.wait()
+    whole.start()
+    first.start()
+    whole.wait()
     for t in range(2):
         stores[t].start()
     first.wait()
     fresh = far_rows(got, cos_ref, sin_ref, blocks)
     for t in range(2):
-        for head in range(edge // HEAD, heads):
-            local_head = head - edge // HEAD
-            lanes = slice(local_head * HEAD, (local_head + 1) * HEAD)
-            overwrite(room.at[2 + t], lanes, phase[head], fresh[t][local_head], slot[late])
+        for head in range(begin, end):
+            here = head - begin
+            lanes = slice(here * HEAD, (here + 1) * HEAD)
+            overwrite(room.at[2 + t], lanes, phase[head], fresh[t][here], slot[late])
         stores[2 + t].start()
     for store in stores:
         store.wait()
@@ -612,34 +606,27 @@
         compiler_params=big,
         cost_estimate=light,
     )(dilation_phase, slots, got, new_cos, new_sin, finals[2], finals[3])
-    return tuple(
-        pl.pallas_call(
-            functools.partial(last_kernel, heads, late, edge),
-            in_specs=[smem, smem, anywhere, vmem, vmem] + [anywhere] * 6,
+    def finish(begin, end, piece, arrays):
+        lanes = slice(begin * HEAD, end * HEAD)
+        size = (end - begin) * HEAD
+        return pl.pallas_call(
+            functools.partial(last_kernel, late, begin, end),
+            in_specs=[smem, smem, anywhere, vmem, vmem] + [anywhere] * 5,
             out_specs=[anywhere] * 4,
             out_shape=[out] * 4,
-            input_output_aliases={7 + t: t for t in range(4)},
+            input_output_aliases={6 + t: t for t in range(4)},
             scratch_shapes=[
-                pltpu.VMEM((devices // 2, 2 * blocks, width - edge), jnp.bfloat16),
-                pltpu.VMEM((4, BLOCK, width - edge), jnp.bfloat16),
+                pltpu.VMEM((devices // 2, 2 * blocks, size), jnp.bfloat16),
+                pltpu.VMEM((4, BLOCK, size), jnp.bfloat16),
                 pltpu.SemaphoreType.DMA(()),
-                pltpu.SemaphoreType.DMA((2,)),
+                pltpu.SemaphoreType.DMA(()),
                 pltpu.SemaphoreType.DMA((4,)),
             ],
             compiler_params=big,
-        )(
-            dilation_phase,
-            slots,
-            got,
-            new_cos[:, edge:],
-            new_sin[:, edge:],
-            parts[late],
-            parts_last[late],
-            finals[0],
-            finals[1],
-            *patched,
-        )
-    )
+        )(dilation_phase, slots, got, new_cos[:, lanes], new_sin[:, lanes], piece, *arrays)
+
+    finals = finish(first, middle, parts[late], [finals[0], finals[1], *patched])
+    return tuple(finish(middle, heads, parts_last[late], finals))
 
 
 def solution(mesh):

time: 150 us -> 150 us (level)
  waiting for transfers between devices: 33 us -> 29 us
  Pallas kernels: 76.1 us -> 78.3 us
    ppermute x12, waiting for transfers between devices: 20.7 us -> 17.5 us  [swap(): return lax.ppermute(array, 'bal', [(i, i ^ k) for i in range(bal_size)])]
    pallas_call x1 -> x2, Pallas kernels: 3 us -> 5.27 us  [finish(): pl.pallas_call(functools.partial(last_kernel, late, begin, end), in_specs...]
  transfers between devices with their start and end apart: 14 -> 14, of which waited for: 9 -> 9; matrix products, arithmetic and copies ran while one was open for 11% -> 12% of each run, Pallas kernels for 47% -> 49%
where the time goes in v3:
time: 150 us; the launch traced here: 149 us
  Pallas kernels  78.3 us (52%)
  waiting for transfers between devices  29 us (19%)
  starting transfers between devices  22.5 us (15%)
  other arithmetic  15.4 us (10%)
  local copies, waits for them, and re-layouts  2.55 us (2%)
    pallas_call x2, Pallas kernels, attend_relaid(): pl.pallas_call(functools.partial(attend_kernel, per_step, blocks, count,...  29.8 us
    pallas_call x2, Pallas kernels, attend_held(): pl.pallas_call(functools.partial(attend_kernel, per_step, blocks, count,...  21.8 us
    ppermute x12, waiting for transfers between devices, swap(): return lax.ppermute(array, 'bal', [(i, i ^ k) for i in range(bal_size)])  17.5 us
    ppermute x12, starting transfers between devices, swap(): return lax.ppermute(array, 'bal', [(i, i ^ k) for i in range(bal_size)])  9.62 us
    all_to_all x1, waiting for transfers between devices, local(): lax.all_to_all(payload.reshape(devices // 2, 2 * blocks, width), ('ctx',...  8.96 us
    pallas_call x2, Pallas kernels, send_inputs(): pl.pallas_call(functools.partial(pack_kernel, jobs, blocks), in_specs=[sm...  7.44 us
    all_to_all x1, starting transfers between devices, local(): lax.all_to_all(payload.reshape(devices // 2, 2 * blocks, width), ('ctx',...  6.85 us
    all_to_all x1, starting transfers between devices, local(): lax.all_to_all(own_far, ('ctx', 'bal'), split_axis=0, concat_axis=0, tile...  5.99 us
  transfers between devices with their start and end apart: 14, of which 9 were waited for; matrix products, arithmetic and copies ran while one was open for 12% of the time, Pallas kernels for 49%

profile of v3, /device:TPU:0, one launch (start us, length us, event | category | flops | bytes accessed | tf_op | source)
XLA Modules:
  0.0 148.7 jit_solution(1209204001663883744)
XLA Ops:
  0.7 2.8 %shard_map.102.after = bf16[4,128,768]{2,1,0:T(8,128)(2,1)} custom-call(s32[128]{0:T(128)} %owner.3, bf16[512,2560]{1,0:T(8,128)(2,1)} %rest_4_.7, bf16[512,2560]{1,0:T(8,128)(2,1)} %rest_4_.7, bf16[512,2560]{1,0:T(8,128)(2,1)} %rest_5_.7, bf16[512,2560]{1,0:T(8,128)(2,1)} %rest_6_.7, bf16[512,2560]{1,0:T(8,128)(2,1)} %rest_7_.7), custom_call_target="tpu_custom_call" | custom-call | tf_op jit(solution)/shard_map/pallas_call | solution.py:383
  3.5 3.0 %collective-permute-start.4 = (bf16[4,128,768]{2,1,0:T(8,128)(2,1)}, bf16[4,128,768]{2,1,0:T(8,128)(2,1)}, u32[]{:S(2)}, u32[]{:S(2)}) collective-permute-start(bf16[4,128,768]{2,1,0:T(8,128)(2,1)} %shard_map.102.after), channel_id=1, source_target_pairs={{0,2},{1,3},{2,0},{3,1},{4,6},{5,7},{6,4},{7,5},{8,10},{9,11},{10,... | collective-permute-start | bytes 2359304 | tf_op jit(solution)/shard_map/ppermute | solution.py:360
  7.0 1.3 fusion.17
  8.3 4.7 %shard_map.103.after = bf16[16,8,2560]{2,1,0:T(8,128)(2,1)} custom-call(s32[20]{0:T(128)} %phase.15, bf16[512,2560]{1,0:T(8,128)(2,1)} %rest_5_.7, bf16[512,2560]{1,0:T(8,128)(2,1)} %rest_6_.7, f32[4,2560]{1,0:T(4,128)} %get-tuple-element.84.cos_ref, f32[4,2560]{1,0:T(4,128)} %get-tuple-element.85.sin_ref, bf16[4,128,768]{2,1,0:T(8,128)(2,1)} %shard_map.102.after), custom_call_target="tpu_custom_call" | custom-call | tf_op jit(solution)/shard_map/pallas_call | solution.py:399
  12.9 6.0 %all-to-all-start = ((bf16[16,8,2560]{2,1,0:T(8,128)(2,1)}), bf16[16,8,2560]{2,1,0:T(8,128)(2,1)}, u32[]{:S(2)}, u32[]{:S(2)}) async-start(bf16[16,8,2560]{2,1,0:T(8,128)(2,1)} %shard_map.103.after), calls=%async_computation | async-start | bytes 1310720 | tf_op jit(solution)/shard_map/all_to_all | solution.py:421
  18.9 4.6 %shard_map.104 = (bf16[4,128,768]{2,1,0:T(8,128)(2,1)}, bf16[4,128,1536]{2,1,0:T(8,128)(2,1)}, bf16[4,128,1536]{2,1,0:T(8,128)(2,1)}) custom-call(s32[128]{0:T(128)} %owner.3, bf16[16,8,2560]{2,1,0:T(8,128)(2,1)} %shard_map.103.after, bf16[512,2560]{1,0:T(8,128)(2,1)} %rest_4_.7, bf16[512,2560]{1,0:T(8,128)(2,1)} %rest_5_.7, bf16[512,2560]{1,0:T(8,128)(2,1)} %rest_6_.7, ...), custom_call_target="tpu_custom_call" | custom-call | tf_op jit(solution)/shard_map/pallas_call | solution.py:383
  23.7 2.0 %collective-permute-start.3 = (bf16[4,128,1536]{2,1,0:T(8,128)(2,1)}, bf16[4,128,1536]{2,1,0:T(8,128)(2,1)}, u32[]{:S(2)}, u32[]{:S(2)}) collective-permute-start(bf16[4,128,1536]{2,1,0:T(8,128)(2,1)} %get-tuple-element.43), channel_id=1, source_target_pairs={{0,3},{1,2},{2,1},{3,0},{4,7},{5,6},{6,5},{7,4},{8,11},{9,10},{10,... | collective-permute-start | bytes 4718600 | tf_op jit(solution)/shard_map/ppermute | solution.py:360
  26.3 2.1 %fusion.13 = (f32[512,64]{1,0:T(8,128)S(1)}, f32[512,64]{1,0:T(8,128)S(1)}, f32[512,64]{1,0:T(8,128)S(1)}, f32[512,64]{1,0:T(8,128)S(1)}, f32[512,64]{1,0:T(8,12...) fusion(f32[64]{0:T(128)S(1)} %get-tuple-element.112, ...), kind=kLoop, calls=%fused_computation.32 | loop fusion | flops 589824 | bytes 1581568 | tf_op jit(solution)/shard_map/neg | solution.py:32
  28.4 0.9 pad_maximum_fusion.rest_8_.rest_0_
  31.3 0.9 pad_maximum_fusion.6.rest_2_
  33.6 2.5 %all-to-all-done = bf16[16,8,2560]{2,1,0:T(8,128)(2,1)} async-done(((bf16[16,8,2560]{2,1,0:T(8,128)(2,1)}), bf16[16,8,2560]{2,1,0:T(8,128)(2,1)}, u32[]{:S(2)}, u32[]{:S(2)}) %all-to-all-start) | async-done | bytes 655392 | tf_op jit(solution)/shard_map/all_to_all | solution.py:421
  37.7 0.9 pad_maximum_fusion.7.rest_3_
  40.1 14.8 %shard_map.105 = (bf16[4,128,768]{2,1,0:T(8,128)(2,1)}, bf16[4,128,768]{2,1,0:T(8,128)(2,1)}, bf16[4,128,768]{2,1,0:T(8,128)(2,1)}, bf16[4,128,768]{2,1,0:T(8,12...) custom-call(s32[8]{0:T(128)} %pad_add_fusion.2.info, s32[20]{0:T(128)} %phase.15, s32[20]{0:T(128)} %seg.7, ...), custom_call_target="tpu_custom_call" | custom-call | flops 20000000000 | bytes 60000000 | tf_op jit(solution)/shard_map/pallas_call | solution.py:465
  55.5 7.0 %shard_map.106 = (bf16[4,128,256]{2,1,0:T(8,128)(2,1)}, bf16[4,128,256]{2,1,0:T(8,128)(2,1)}, bf16[4,128,256]{2,1,0:T(8,128)(2,1)}, bf16[4,128,256]{2,1,0:T(8,12...) custom-call(s32[8]{0:T(128)} %pad_add_fusion.2.info, ...), custom_call_target="tpu_custom_call", output_to_operand_aliasing={{4}: (15, {}), {5}: (16, {})} | custom-call | flops 20000000000 | bytes 60000000 | tf_op jit(solution)/shard_map/pallas_call | solution.py:465
  62.5 2.6 %collective-permute-done.3.rest_10_ = bf16[4,128,1536]{2,1,0:T(8,128)(2,1)} collective-permute-done((bf16[4,128,1536]{2,1,0:T(8,128)(2,1)}, bf16[4,128,1536]{2,1,0:T(8,128)(2,1)}, u32[]{:S(2)}, u32[]{:S(2)}) %collective-permute-start.3) | collective-permute-done | bytes 1572896 | tf_op jit(solution)/shard_map/ppermute | solution.py:360
  65.1 15.0 %shard_map.107 = (bf16[4,128,2560]{2,1,0:T(8,128)(2,1)}, bf16[4,128,2560]{2,1,0:T(8,128)(2,1)}, bf16[4,128,2560]{2,1,0:T(8,128)(2,1)}, bf16[4,128,2560]{2,1,0:T(...) custom-call(s32[12]{0:T(128)} %pad_add_fusion.1.info, ...), custom_call_target="tpu_custom_call", output_to_operand_aliasing={{4}: (18, {}), {5}: (19, {})} | custom-call | flops 2000000000 | bytes 5000000 | tf_op jit(solution)/shard_map/pallas_call | solution.py:516
  80.1 2.3 %collective-permute-done.2.rest_9_ = bf16[4,128,768]{2,1,0:T(8,128)(2,1)} collective-permute-done((bf16[4,128,768]{2,1,0:T(8,128)(2,1)}, bf16[4,128,768]{2,1,0:T(8,128)(2,1)}, u32[]{:S(2)}, u32[]{:S(2)}) %collective-permute-start.2) | collective-permute-done | bytes 786464 | tf_op jit(solution)/shard_map/ppermute | solution.py:360
  82.4 14.8 %shard_map.108 = (bf16[4,128,2560]{2,1,0:T(8,128)(2,1)}, bf16[4,128,2560]{2,1,0:T(8,128)(2,1)}, bf16[4,128,2560]{2,1,0:T(8,128)(2,1)}, bf16[4,128,2560]{2,1,0:T(...) custom-call(s32[12]{0:T(128)} %pad_add_fusion.1.info, ...), custom_call_target="tpu_custom_call", output_to_operand_aliasing={{0}: (18, {}), {1}: (19, {}), {2}: (20, {}), {3}: (21, {}),... | custom-call | flops 2000000000 | bytes 5000000 | tf_op jit(solution)/shard_map/pallas_call | solution.py:516
  97.2 1.8 %collective-permute-done.5.refs_1_.rest_2_ = bf16[4,128,768]{2,1,0:T(8,128)(2,1)} collective-permute-done((bf16[4,128,768]{2,1,0:T(8,128)(2,1)}, bf16[4,128,768]{2,1,0:T(8,128)(2,1)}, u32[]{:S(2)}, u32[]{:S(2)}) %collective-permute-start.5) | collective-permute-done | bytes 786464 | tf_op jit(solution)/shard_map/ppermute | solution.py:360
  99.1 1.4 collective-permute-start.7
  100.5 0.9 collective-permute-done.6
  101.4 2.1 %add_convert_fusion.refs_0_ = bf16[128,2560]{1,0:T(8,128)(2,1)} fusion(bf16[128,2560]{1,0:T(8,128)(2,1)S(1)} %collective-permute-done.6, bf16[128,2560]{1,0:T(8,128)(2,1)} %get-tuple-element.54), kind=kLoop, calls=%fused_computation | loop fusion | flops 1310720 | bytes 1966080 | tf_op jit(solution)/shard_map/convert_element_type | solution.py:564
  103.5 4.7 %collective-permute-done.7.refs_1_.rest_5_ = bf16[4,128,256]{2,1,0:T(8,128)(2,1)} collective-permute-done((bf16[4,128,256]{2,1,0:T(8,128)(2,1)}, bf16[4,128,256]{2,1,0:T(8,128)(2,1)}, u32[]{:S(2)}, u32[]{:S(2)}) %collective-permute-start.7) | collective-permute-done | bytes 262176 | tf_op jit(solution)/shard_map/ppermute | solution.py:360
  108.1 6.9 %all-to-all-start.1 = ((bf16[16,8,2560]{2,1,0:T(8,128)(2,1)}), bf16[16,8,2560]{2,1,0:T(8,128)(2,1)}, u32[]{:S(2)}, u32[]{:S(2)}) async-start(bf16[16,8,2560]{2,1,0:T(8,128)(2,1)} %bitcast.56), calls=%async_computation.1 | async-start | bytes 1310720 | tf_op jit(solution)/shard_map/all_to_all | solution.py:565
  115.1 1.9 %collective-permute-start.9 = (bf16[4,128,768]{2,1,0:T(8,128)(2,1)}, bf16[4,128,768]{2,1,0:T(8,128)(2,1)}, u32[]{:S(2)}, u32[]{:S(2)}) collective-permute-start(bf16[4,128,768]{2,1,0:T(8,128)(2,1)} %get-tuple-element.59), channel_id=1, source_target_pairs={{0,3},{1,2},{2,1},{3,0},{4,7},{5,6},{6,5},{7,4},{8,11},{9,10},{10,... | collective-permute-start | bytes 2359304 | tf_op jit(solution)/shard_map/ppermute | solution.py:360
  119.7 3.7 %shard_map.111 = (bf16[512,2560]{1,0:T(8,128)(2,1)}, bf16[512,2560]{1,0:T(8,128)(2,1)}, bf16[512,2560]{1,0:T(8,128)(2,1)}, bf16[512,2560]{1,0:T(8,128)(2,1)}) custom-call(s32[4]{0:T(128)} %copy-done.3, bf16[4,128,768]{2,1,0:T(8,128)(2,1)} %get-tuple-element.60.rest_0_, ...), custom_call_target="tpu_custom_call", output_to_operand_aliasing={{0}: (7, {}), {1}: (8, {}), {2}: (9, {}), {3}: (10, {})} | custom-call | flops 2000000000 | bytes 5000000 | tf_op jit(solution)/shard_map/pallas_call | solution.py:581
  123.4 9.0 %all-to-all-done.1.got_hbm = bf16[16,8,2560]{2,1,0:T(8,128)(2,1)} async-done(((bf16[16,8,2560]{2,1,0:T(8,128)(2,1)}), bf16[16,8,2560]{2,1,0:T(8,128)(2,1)}, u32[]{:S(2)}, u32[]{:S(2)}) %all-to-all-start.1) | async-done | bytes 655392 | tf_op jit(solution)/shard_map/all_to_all | solution.py:565
  132.4 5.7 %shard_map.112 = (bf16[512,2560]{1,0:T(8,128)(2,1)}, bf16[512,2560]{1,0:T(8,128)(2,1)}) custom-call(s32[20]{0:T(128)} %phase.15, s32[4]{0:T(128)} %copy-done.3, bf16[16,8,2560]{2,1,0:T(8,128)(2,1)} %all-to-all-done.1.got_hbm, f32[4,2560]{1,0:T(4,128)} %copy-done.1, f32[4,2560]{1,0:T(4,128)} %copy-done, ...), custom_call_target="tpu_custom_call", output_to_operand_aliasing={{0}: (5, {}), {1}: (6, {})} | custom-call | flops 2000000000 | bytes 5000000 | tf_op jit(solution)/shard_map/pallas_call | solution.py:593
  138.1 2.4 %collective-permute-done.9.piece = bf16[4,128,768]{2,1,0:T(8,128)(2,1)} collective-permute-done((bf16[4,128,768]{2,1,0:T(8,128)(2,1)}, bf16[4,128,768]{2,1,0:T(8,128)(2,1)}, u32[]{:S(2)}, u32[]{:S(2)}) %collective-permute-start.9) | collective-permute-done | bytes 786464 | tf_op jit(solution)/shard_map/ppermute | solution.py:360
  140.5 2.8 %shard_map.113 = (bf16[512,2560]{1,0:T(8,128)(2,1)}, bf16[512,2560]{1,0:T(8,128)(2,1)}, bf16[512,2560]{1,0:T(8,128)(2,1)}, bf16[512,2560]{1,0:T(8,128)(2,1)}) custom-call(s32[20]{0:T(128)} %phase.15, s32[4]{0:T(128)} %copy-done.3, ...), custom_call_target="tpu_custom_call", output_to_operand_aliasing={{0}: (6, {}), {1}: (7, {}), {2}: (8, {}), {3}: (9, {})} | custom-call | tf_op jit(solution)/shard_map/pallas_call | solution.py:612
  143.3 2.8 %collective-permute-done.8.piece = bf16[4,128,256]{2,1,0:T(8,128)(2,1)} collective-permute-done((bf16[4,128,256]{2,1,0:T(8,128)(2,1)}, bf16[4,128,256]{2,1,0:T(8,128)(2,1)}, u32[]{:S(2)}, u32[]{:S(2)}) %collective-permute-start.8) | collective-permute-done | bytes 262176 | tf_op jit(solution)/shard_map/ppermute | solution.py:360
  146.1 2.4 %shard_map.114 = (bf16[512,2560]{1,0:T(8,128)(2,1)}, bf16[512,2560]{1,0:T(8,128)(2,1)}, bf16[512,2560]{1,0:T(8,128)(2,1)}, bf16[512,2560]{1,0:T(8,128)(2,1)}) custom-call(s32[20]{0:T(128)} %phase.15, s32[4]{0:T(128)} %copy-done.3, ...), custom_call_target="tpu_custom_call", output_to_operand_aliasing={{0}: (6, {}), {1}: (7, {}), {2}: (8, {}), {3}: (9, {})} | custom-call | tf_op jit(solution)/shard_map/pallas_call | solution.py:612
  (62 shorter events, 11.2 us)
Async XLA Ops:
  0.6 5.9 %copy-start.4 = (s32[128]{0:T(128)S(1)}, s32[128]{0:T(128)}, u32[]{:S(2)}) copy-start(s32[128]{0:T(128)} %owner.3) | copy-start | bytes 1540
  0.6 6.1 %copy-start.2 = (s32[20]{0:T(128)S(1)}, s32[20]{0:T(128)}, u32[]{:S(2)}) copy-start(s32[20]{0:T(128)} %phase.15) | copy-start | bytes 244
  3.5 36.7 %collective-permute-start.4 = (bf16[4,128,768]{2,1,0:T(8,128)(2,1)}, bf16[4,128,768]{2,1,0:T(8,128)(2,1)}, u32[]{:S(2)}, u32[]{:S(2)}) collective-permute-start(bf16[4,128,768]{2,1,0:T(8,128)(2,1)} %shard_map.102.after), channel_id=1, source_target_pairs={{0,2},{1,3},{2,0},{3,1},{4,6},{5,7},{6,4},{7,5},{8,10},{9,11},{10,... | collective-permute-start | bytes 2359304 | tf_op jit(solution)/shard_map/ppermute | solution.py:360
  8.2 109.4 %copy-start.1 = (f32[4,2560]{1,0:T(4,128)}, f32[4,2560]{1,0:T(4,128)S(1)}, u32[]{:S(2)}) copy-start(f32[4,2560]{1,0:T(4,128)S(1)} %get-tuple-element.81.cos_ref) | copy-start | bytes 122884
  8.2 110.6 %copy-start = (f32[4,2560]{1,0:T(4,128)}, f32[4,2560]{1,0:T(4,128)S(1)}, u32[]{:S(2)}) copy-start(f32[4,2560]{1,0:T(4,128)S(1)} %get-tuple-element.80.sin_ref) | copy-start | bytes 122884
  12.9 23.2 %all-to-all-start = ((bf16[16,8,2560]{2,1,0:T(8,128)(2,1)}), bf16[16,8,2560]{2,1,0:T(8,128)(2,1)}, u32[]{:S(2)}, u32[]{:S(2)}) async-start(bf16[16,8,2560]{2,1,0:T(8,128)(2,1)} %shard_map.103.after), calls=%async_computation | async-start | bytes 1310720 | tf_op jit(solution)/shard_map/all_to_all | solution.py:421
  23.6 5.7 %copy-start.5 = (s32[128]{0:T(128)S(1)}, s32[128]{0:T(128)}, u32[]{:S(2)}) copy-start(s32[128]{0:T(128)} %owner.3) | copy-start | bytes 1540
  23.6 16.5 %collective-permute-start.1 = (bf16[4,128,1536]{2,1,0:T(8,128)(2,1)}, bf16[4,128,1536]{2,1,0:T(8,128)(2,1)}, u32[]{:S(2)}, u32[]{:S(2)}) collective-permute-start(bf16[4,128,1536]{2,1,0:T(8,128)(2,1)} %get-tuple-element.41), channel_id=1, source_target_pairs={{0,1},{1,0},{2,3},{3,2},{4,5},{5,4},{6,7},{7,6},{8,9},{9,8},{10,11... | collective-permute-start | bytes 4718600 | tf_op jit(solution)/shard_map/ppermute | solution.py:360
  23.7 41.5 %collective-permute-start.3 = (bf16[4,128,1536]{2,1,0:T(8,128)(2,1)}, bf16[4,128,1536]{2,1,0:T(8,128)(2,1)}, u32[]{:S(2)}, u32[]{:S(2)}) collective-permute-start(bf16[4,128,1536]{2,1,0:T(8,128)(2,1)} %get-tuple-element.43), channel_id=1, source_target_pairs={{0,3},{1,2},{2,1},{3,0},{4,7},{5,6},{6,5},{7,4},{8,11},{9,10},{10,... | collective-permute-start | bytes 4718600 | tf_op jit(solution)/shard_map/ppermute | solution.py:360
  25.7 56.8 %collective-permute-start.2 = (bf16[4,128,768]{2,1,0:T(8,128)(2,1)}, bf16[4,128,768]{2,1,0:T(8,128)(2,1)}, u32[]{:S(2)}, u32[]{:S(2)}) collective-permute-start(bf16[4,128,768]{2,1,0:T(8,128)(2,1)} %get-tuple-element.42), channel_id=1, source_target_pairs={{0,2},{1,3},{2,0},{3,1},{4,6},{5,7},{6,4},{7,5},{8,10},{9,11},{10,... | collective-permute-start | bytes 2359304 | tf_op jit(solution)/shard_map/ppermute | solution.py:360
  26.3 6.7 %copy-start.3 = (s32[4]{0:T(128)}, s32[4]{0:T(128)S(1)}, u32[]{:S(2)}) copy-start(s32[4]{0:T(128)S(1)} %iota_xor_fusion.slot) | copy-start | bytes 52
  36.2 4.0 %collective-permute-start = (bf16[128,2560]{1,0:T(8,128)(2,1)}, bf16[128,2560]{1,0:T(8,128)(2,1)}, u32[]{:S(2)}, u32[]{:S(2)}) collective-permute-start(bf16[128,2560]{1,0:T(8,128)(2,1)} %bitcast.far_ref), channel_id=1, source_target_pairs={{0,1},{1,0},{2,3},{3,2},{4,5},{5,4},{6,7},{7,6},{8,9},{9,8},{10,11... | collective-permute-start | bytes 1966088 | tf_op jit(solution)/shard_map/ppermute | solution.py:360
  54.9 44.2 %collective-permute-start.5 = (bf16[4,128,768]{2,1,0:T(8,128)(2,1)}, bf16[4,128,768]{2,1,0:T(8,128)(2,1)}, u32[]{:S(2)}, u32[]{:S(2)}) collective-permute-start(bf16[4,128,768]{2,1,0:T(8,128)(2,1)} %get-tuple-element.56), channel_id=1, source_target_pairs={{0,2},{1,3},{2,0},{3,1},{4,6},{5,7},{6,4},{7,5},{8,10},{9,11},{10,... | collective-permute-start | bytes 2359304 | tf_op jit(solution)/shard_map/ppermute | solution.py:360
  99.1 2.3 %collective-permute-start.6 = (bf16[128,2560]{1,0:T(8,128)(2,1)}, bf16[128,2560]{1,0:T(8,128)(2,1)S(1)}, u32[]{:S(2)}, u32[]{:S(2)}) collective-permute-start(bf16[128,2560]{1,0:T(8,128)(2,1)} %shard_map.109), channel_id=1, source_target_pairs={{0,1},{1,0},{2,3},{3,2},{4,5},{5,4},{6,7},{7,6},{8,9},{9,8},{10,11... | collective-permute-start | bytes 1966088 | tf_op jit(solution)/shard_map/ppermute | solution.py:360
  99.1 9.0 %collective-permute-start.7 = (bf16[4,128,256]{2,1,0:T(8,128)(2,1)}, bf16[4,128,256]{2,1,0:T(8,128)(2,1)}, u32[]{:S(2)}, u32[]{:S(2)}) collective-permute-start(bf16[4,128,256]{2,1,0:T(8,128)(2,1)} %get-tuple-element.57), channel_id=1, source_target_pairs={{0,2},{1,3},{2,0},{3,1},{4,6},{5,7},{6,4},{7,5},{8,10},{9,11},{10,... | collective-permute-start | bytes 786440 | tf_op jit(solution)/shard_map/ppermute | solution.py:360
  108.1 24.2 %all-to-all-start.1 = ((bf16[16,8,2560]{2,1,0:T(8,128)(2,1)}), bf16[16,8,2560]{2,1,0:T(8,128)(2,1)}, u32[]{:S(2)}, u32[]{:S(2)}) async-start(bf16[16,8,2560]{2,1,0:T(8,128)(2,1)} %bitcast.56), calls=%async_computation.1 | async-start | bytes 1310720 | tf_op jit(solution)/shard_map/all_to_all | solution.py:565
  115.0 4.7 %collective-permute-start.10 = (bf16[4,128,768]{2,1,0:T(8,128)(2,1)}, bf16[4,128,768]{2,1,0:T(8,128)(2,1)}, u32[]{:S(2)}, u32[]{:S(2)}) collective-permute-start(bf16[4,128,768]{2,1,0:T(8,128)(2,1)} %get-tuple-element.61), channel_id=1, source_target_pairs={{0,1},{1,0},{2,3},{3,2},{4,5},{5,4},{6,7},{7,6},{8,9},{9,8},{10,11... | collective-permute-start | bytes 2359304 | tf_op jit(solution)/shard_map/ppermute | solution.py:360
  115.1 25.4 %collective-permute-start.9 = (bf16[4,128,768]{2,1,0:T(8,128)(2,1)}, bf16[4,128,768]{2,1,0:T(8,128)(2,1)}, u32[]{:S(2)}, u32[]{:S(2)}) collective-permute-start(bf16[4,128,768]{2,1,0:T(8,128)(2,1)} %get-tuple-element.59), channel_id=1, source_target_pairs={{0,3},{1,2},{2,1},{3,0},{4,7},{5,6},{6,5},{7,4},{8,11},{9,10},{10,... | collective-permute-start | bytes 2359304 | tf_op jit(solution)/shard_map/ppermute | solution.py:360
  117.0 2.7 %collective-permute-start.11 = (bf16[4,128,256]{2,1,0:T(8,128)(2,1)}, bf16[4,128,256]{2,1,0:T(8,128)(2,1)}, u32[]{:S(2)}, u32[]{:S(2)}) collective-permute-start(bf16[4,128,256]{2,1,0:T(8,128)(2,1)} %get-tuple-element.63), channel_id=1, source_target_pairs={{0,1},{1,0},{2,3},{3,2},{4,5},{5,4},{6,7},{7,6},{8,9},{9,8},{10,11... | collective-permute-start | bytes 786440 | tf_op jit(solution)/shard_map/ppermute | solution.py:360
  119.4 26.7 %collective-permute-start.8 = (bf16[4,128,256]{2,1,0:T(8,128)(2,1)}, bf16[4,128,256]{2,1,0:T(8,128)(2,1)}, u32[]{:S(2)}, u32[]{:S(2)}) collective-permute-start(bf16[4,128,256]{2,1,0:T(8,128)(2,1)} %get-tuple-element.58), channel_id=1, source_target_pairs={{0,3},{1,2},{2,1},{3,0},{4,7},{5,6},{6,5},{7,4},{8,11},{9,10},{10,... | collective-permute-start | bytes 786440 | tf_op jit(solution)/shard_map/ppermute | solution.py:360
